TPU v7x, 512 devices: a whole 4x4x16 slice. The times are simulated.
512 devices in a mesh: roll: 16 (over z), fsdp: 32 (over x, y, core).
Axes of the slice: x: 4, y: 4, z: 16, core: 2. Of those that a mesh axis runs over, the one named last changes fastest.
Arguments:
- hidden_rows: bfloat16 [256, 5120], P('roll', 'fsdp'), may hold values from -6 to 6
- embed_rows: bfloat16 [256, 5120], P('roll', 'fsdp'), may hold values from -6 to 6
- target_rows: bfloat16 [256, 5120], P('roll'), may hold values from -6 to 6
- counts: int32 [16], P('roll'), may hold values from 1 to 16, 128 in all
- fc_weight: bfloat16 [2, 5120, 5120], P(None, 'fsdp', 'roll'), may hold values from -0.0625 to 0.0625
- norm_gain: float32 [5120], P('roll'), may hold values from 0.35 to 15
- gate_weight: bfloat16 [5120, 25600], P('roll', 'fsdp'), may hold values from -0.078125 to 0.078125
- up_weight: bfloat16 [5120, 25600], P('roll', 'fsdp'), may hold values from -0.078125 to 0.078125
- down_weight: bfloat16 [25600, 5120], P('fsdp', 'roll'), may hold values from -0.0390625 to 0.0390625
Outputs:
- grad_fc: float32 [2, 5120, 5120], P(None, 'fsdp', 'roll')
- grad_gain: float32 [5120], P('roll')
- grad_gate: bfloat16 [5120, 25600], P('roll', 'fsdp')
- grad_up: bfloat16 [5120, 25600], P('roll', 'fsdp')
- grad_down: float32 [25600, 5120], P('fsdp', 'roll')
Inputs may be any that keep to these rules, and one draw needn't show every extreme that they name: counts[e] of engine e's slots, its first ones, hold live rows; the counts sum to 128 and the largest equals 16.
All inputs are finite; a program needn't handle non-finite values. No bound on the sum of `counts` on one device may be relied on, other than what follows from the above.
Results may differ from a plain program's by a relative error of at most 0.012.
Values may be sent and summed in bfloat16 or wider, within the bound.
A program may use at most 64 MiB of HBM per device.

v0:
```python
import math

import jax
import jax.numpy as jnp
from jax import lax
from jax.sharding import PartitionSpec as P

D = 5120
ROW_ENG = 8


epsilon = 1e-06


def shards(
    hidden_rows,
    embed_rows,
    target_rows,
    counts,
    fc_weight,
    norm_gain,
    gate_weight,
    up_weight,
    down_weight,
):
    engines = lax.axis_size("roll")
    capacity = hidden_rows.shape[0]
    live_total = ROW_ENG * engines
    loss_scale = 1.0 / math.sqrt(live_total)
    everyone = lax.all_gather(counts, "roll", axis=0, tiled=True)
    embeds, hiddens = (
        lax.all_gather(embed_rows, "roll", axis=0, tiled=True),
        lax.all_gather(hidden_rows, "roll", axis=0, tiled=True),
    )
    targets = lax.all_to_all(target_rows, "roll", split_axis=1, concat_axis=0, tiled=True)
    slot_ids = jnp.arange(engines * capacity, dtype=jnp.int32)
    slot_engine = slot_ids // capacity
    matches = slot_engine[:, None] == jnp.arange(engines, dtype=jnp.int32)[None, :]
    slot_limit = jnp.sum(jnp.where(matches, everyone[None, :], 0), axis=1)
    live_mask = (slot_ids % capacity < slot_limit).astype(jnp.float32)[:, None]
    fc_part = jnp.dot(embeds, fc_weight[0], preferred_element_type=jnp.float32) + jnp.dot(
        hiddens, fc_weight[1], preferred_element_type=jnp.float32
    )
    mixed_in = lax.psum(fc_part, "fsdp")
    squares = lax.psum(jnp.sum(mixed_in * mixed_in, axis=1), "roll")
    inverse_rms = lax.rsqrt(squares[:, None] / D + epsilon)
    normed = (mixed_in * inverse_rms * norm_gain).astype(jnp.bfloat16)
    gate_pre, up_pre = lax.psum(
        (
            jnp.dot(normed, gate_weight, preferred_element_type=jnp.float32),
            jnp.dot(normed, up_weight, preferred_element_type=jnp.float32),
        ),
        "roll",
    )
    activated = (jax.nn.silu(gate_pre) * up_pre).astype(jnp.bfloat16)
    down_out = lax.psum(jnp.dot(activated, down_weight, preferred_element_type=jnp.float32), "fsdp")
    drafted = mixed_in + down_out
    loss_grad = (drafted - targets.astype(jnp.float32)) * loss_scale * live_mask
    loss_grad_b = loss_grad.astype(jnp.bfloat16)
    grad_down = jnp.einsum("rf,rd->fd", activated, loss_grad_b, preferred_element_type=jnp.float32)
    back_act = lax.psum(
        jnp.einsum("rd,fd->rf", loss_grad_b, down_weight, preferred_element_type=jnp.float32),
        "roll",
    )
    sigmoid_gate = jax.nn.sigmoid(gate_pre)
    back_gate = (back_act * up_pre * sigmoid_gate * (1.0 + gate_pre * (1.0 - sigmoid_gate))).astype(
        jnp.bfloat16
    )
    back_up = (back_act * gate_pre * sigmoid_gate).astype(jnp.bfloat16)
    grad_gate = jnp.einsum(
        "rd,rf->df", normed, back_gate, preferred_element_type=jnp.float32
    ).astype(jnp.bfloat16)
    grad_up = jnp.einsum("rd,rf->df", normed, back_up, preferred_element_type=jnp.float32).astype(
        jnp.bfloat16
    )
    norm_terms = jnp.einsum(
        "rf,df->rd", back_gate, gate_weight, preferred_element_type=jnp.float32
    ) + jnp.einsum("rf,df->rd", back_up, up_weight, preferred_element_type=jnp.float32)
    back_norm = lax.psum(norm_terms, "fsdp")
    grad_gain = jnp.sum(back_norm * mixed_in * inverse_rms, axis=0)
    gained = back_norm * norm_gain
    inner = lax.psum(jnp.sum(gained * mixed_in, axis=1), "roll")[:, None] / D
    back_mix = loss_grad + inverse_rms * gained - mixed_in * inverse_rms**3 * inner
    back_mix_b = back_mix.astype(jnp.bfloat16)
    grad_fc = jnp.stack(
        [
            jnp.einsum("rk,rd->kd", embeds, back_mix_b, preferred_element_type=jnp.float32),
            jnp.einsum("rk,rd->kd", hiddens, back_mix_b, preferred_element_type=jnp.float32),
        ]
    )
    return (grad_fc, grad_gain, grad_gate, grad_up, grad_down)


def solution(mesh):
    placed = (
        P("roll", "fsdp"),
        P("roll", "fsdp"),
        P("roll", None),
        P("roll"),
        P(None, "fsdp", "roll"),
        P("roll"),
        P("roll", "fsdp"),
        P("roll", "fsdp"),
        P("fsdp", "roll"),
    )
    return jax.shard_map(
        shards,
        mesh=mesh,
        in_specs=placed,
        out_specs=(
            P(None, "fsdp", "roll"),
            P("roll"),
            P("roll", "fsdp"),
            P("roll", "fsdp"),
            P("fsdp", "roll"),
        ),
        check_vma=False,
    )
```

profile of v0, /device:TPU:1, one launch (start us, length us, event | category | flops | bytes accessed | tf_op | source)
XLA Modules:
  0.0 822.4 jit_solution(18159155885221375472)
XLA Ops:
  7.2 0.0 copy-start
  7.2 0.0 all-reduce.8.cloned.1.call-start
  7.2 30.2 %all_gather.9 = bf16[256,160]{1,0:T(8,128)(2,1)S(1)} all-gather(bf16[16,160]{1,0:T(8,128)(2,1)} %param.10), channel_id=1, replica_groups=mesh['roll'=16,'fsdp'=32] {'roll'}, dimensions={0}, use_global_device_ids=true | all-gather | bytes 87040 | tf_op jit(solution)/shard_map/all_gather | solution.py:32
  37.4 20.1 %all_gather.10 = bf16[256,160]{1,0:T(8,128)(2,1)S(1)} all-gather(bf16[16,160]{1,0:T(8,128)(2,1)} %param.9), channel_id=1, replica_groups=mesh['roll'=16,'fsdp'=32] {'roll'}, dimensions={0}, use_global_device_ids=true | all-gather | bytes 87040 | tf_op jit(solution)/shard_map/all_gather | solution.py:33
  57.5 0.0 copy-done.12
  57.5 1.2 fusion.1
  58.7 0.0 copy-start.4
  58.8 1.9 convolution_add_fusion
  60.7 0.0 all-reduce.8.cloned.1.call-update
  60.7 0.0 copy-start.6
  60.7 0.0 all-reduce.16.cloned.1.call-start
  60.8 143.7 %all-reduce.8.cloned.1.call-done = f32[256,320]{0,1:T(8,128)} async-done(((f32[256,320]{0,1:T(8,128)}), f32[256,320]{0,1:T(8,128)}) %all-reduce.8.cloned.1.call-update) | async-done | bytes 327696 | tf_op jit(solution)/shard_map/psum | solution.py:44
  204.5 1.0 multiply_reduce_fusion.2
  205.5 24.7 %psum.57 = f32[256]{0:T(256)S(1)} all-reduce(f32[256]{0:T(256)S(1)} %multiply_reduce_fusion.2), channel_id=1, replica_groups=mesh['roll'=16,'fsdp'=32] {'roll'}, use_global_device_ids=true, to_apply=%region_2.3 | all-reduce | flops 256 | bytes 2048 | tf_op jit(solution)/shard_map/psum | solution.py:45
  230.2 0.0 copy-done.10
  230.2 0.0 copy-done.15
  230.2 1.1 multiply_convert_fusion.3
  231.3 0.0 copy-done.4
  231.3 1.3 fusion.7
  232.6 0.0 copy-done.6
  232.6 1.3 fusion.8
  234.0 0.0 all-reduce.16.cloned.1.call-update
  234.0 0.9 copy-done.14
  234.9 0.2 all_to_all.10
  235.0 0.7 copy.17
  235.8 8.0 all-to-all-start
  243.7 0.0 all-reduce.10.cloned.1.call-start
  244.4 1.3 dynamic-slice
  245.7 0.8 dynamic-update-slice
  246.5 19.2 %all-reduce = s32[16]{0:T(128)S(1)} all-reduce(s32[16]{0:T(128)S(1)} %dynamic-update-slice), channel_id=1, replica_groups=mesh['roll'=16,'fsdp'=32] {'roll'}, use_global_device_ids=true, to_apply=%add | all-reduce | flops 16 | bytes 128
  265.6 0.1 select_reduce_fusion
  265.7 104.6 %all-reduce.16.cloned.1.call-done = (f32[256,800]{0,1:T(8,128)}, f32[256,800]{0,1:T(8,128)}) async-done(((f32[256,800]{0,1:T(8,128)}, f32[256,800]{0,1:T(8,128)}), (f32[256,800]{0,1:T(8,128)}, f32[256,800]{0,1:T(8,128)})) %all-reduce.16.cloned.1.call-update) | async-done | bytes 1638416 | tf_op jit(solution)/shard_map/psum | solution.py:48
  370.4 1.6 multiply_convert_fusion.2
  372.0 0.0 copy-done
  372.0 1.1 fusion.11
  373.1 0.0 all-reduce.10.cloned.1.call-update
  373.1 0.0 all-reduce.12.cloned.1.call-start
  373.1 0.0 all-to-all-done
  373.2 0.1 copy.18
  373.3 139.3 %all-reduce.10.cloned.1.call-done = f32[256,320]{0,1:T(8,128)} async-done(((f32[256,320]{0,1:T(8,128)}), f32[256,320]{0,1:T(8,128)}) %all-reduce.10.cloned.1.call-update) | async-done | bytes 327696 | tf_op jit(solution)/shard_map/psum | solution.py:56
  512.7 0.0 copy-done.1
  512.7 1.0 fusion.5
  513.7 0.0 copy-start.8
  513.7 0.7 copy-done.8
  514.4 1.3 fusion.9
  515.7 0.0 all-reduce.12.cloned.1.call-update
  515.8 0.0 all-reduce.14.cloned.1.call-start
  515.8 2.4 fusion.10
  518.2 125.8 %all-reduce.12.cloned.1.call-done = f32[256,800]{0,1:T(8,128)} async-done(((f32[256,800]{0,1:T(8,128)}), f32[256,800]{0,1:T(8,128)}) %all-reduce.12.cloned.1.call-update) | async-done | bytes 819216 | tf_op jit(solution)/shard_map/psum | solution.py:61
  644.0 1.6 multiply_convert_fusion
  645.6 0.0 copy-start.7
  645.6 0.3 fusion.12
  646.0 1.2 convolution_convert_fusion.1
  647.2 1.1 convolution_add_fusion.1
  648.2 0.0 all-reduce.14.cloned.1.call-update
  648.2 1.2 convolution_convert_fusion
  649.4 137.4 %all-reduce.14.cloned.1.call-done = f32[256,320]{0,1:T(8,128)} async-done(((f32[256,320]{0,1:T(8,128)}), f32[256,320]{0,1:T(8,128)}) %all-reduce.14.cloned.1.call-update) | async-done | bytes 327696 | tf_op jit(solution)/shard_map/psum | solution.py:79
  786.8 1.8 multiply_reduce_fusion
  788.6 24.8 %psum.63 = f32[256]{0:T(256)S(1)} all-reduce(f32[256]{0:T(256)S(1)} %get-tuple-element.6), channel_id=1, replica_groups=mesh['roll'=16,'fsdp'=32] {'roll'}, use_global_device_ids=true, to_apply=%region_10.11 | all-reduce | flops 256 | bytes 2048 | tf_op jit(solution)/shard_map/psum | solution.py:82
  813.4 0.0 copy-done.9
  813.4 1.1 subtract_convert_fusion
  814.5 0.2 convolution_bitcast_fusion
  814.8 0.2 convolution_bitcast_fusion.1
  815.0 0.8 pad_maximum_fusion
  (23 shorter events, 0.1 us)
Async XLA Ops:
  7.2 364.8 %copy-start = (bf16[800,320]{0,1:T(8,128)(2,1)S(1)}, bf16[800,320]{0,1:T(8,128)(2,1)}, u32[]{:S(2)}) copy-start(bf16[800,320]{0,1:T(8,128)(2,1)} %param.17) | copy-start | bytes 1536004
  7.2 197.3 %all-reduce.8.cloned.1.call-start = ((), (), s32[]{:S(2)}) async-start(), calls=%async_computation.1 | async-start | bytes 655360 | tf_op jit(solution)/shard_map/psum | solution.py:44
  37.4 20.1 %copy-start.12 = (bf16[256,160]{1,0:T(8,128)(2,1)}, bf16[256,160]{1,0:T(8,128)(2,1)S(1)}, u32[]{:S(2)}) copy-start(bf16[256,160]{1,0:T(8,128)(2,1)S(1)} %all_gather.9) | copy-start | bytes 245764
  37.4 192.8 %copy-start.15 = (f32[320]{0:T(512)S(1)}, f32[320]{0:T(512)}, u32[]{:S(2)}) copy-start(f32[320]{0:T(512)} %param.14) | copy-start | bytes 3844
  57.5 172.7 %copy-start.10 = (bf16[256,160]{1,0:T(8,128)(2,1)}, bf16[256,160]{1,0:T(8,128)(2,1)S(1)}, u32[]{:S(2)}) copy-start(bf16[256,160]{1,0:T(8,128)(2,1)S(1)} %all_gather.10) | copy-start | bytes 245764
  58.7 172.6 %copy-start.4 = (bf16[320,800]{1,0:T(8,128)(2,1)S(1)}, bf16[320,800]{1,0:T(8,128)(2,1)}, u32[]{:S(2)}) copy-start(bf16[320,800]{1,0:T(8,128)(2,1)} %param.15) | copy-start | bytes 1536004
  60.7 171.9 %copy-start.6 = (bf16[320,800]{1,0:T(8,128)(2,1)S(1)}, bf16[320,800]{1,0:T(8,128)(2,1)}, u32[]{:S(2)}) copy-start(bf16[320,800]{1,0:T(8,128)(2,1)} %param.16) | copy-start | bytes 1536004
  60.7 309.6 %all-reduce.16.cloned.1.call-start = ((), (), s32[]{:S(2)}) async-start(), calls=%async_computation.5 | async-start | bytes 3276800 | tf_op jit(solution)/shard_map/psum | solution.py:48
  234.0 0.9 copy-start.14
  235.8 137.4 %all-to-all-start = ((bf16[16,16,320]{2,0,1:T(8,128)(2,1)}), bf16[16,16,320]{2,0,1:T(8,128)(2,1)S(1)}, u32[]{:S(2)}, u32[]{:S(2)}) async-start(bf16[16,16,320]{2,0,1:T(8,128)(2,1)} %copy.17), calls=%async_computation | async-start | bytes 393216 | tf_op jit(solution)/shard_map/all_to_all | solution.py:35
  243.7 269.0 %all-reduce.10.cloned.1.call-start = ((), (), s32[]{:S(2)}) async-start(), calls=%async_computation.2 | async-start | bytes 655360 | tf_op jit(solution)/shard_map/psum | solution.py:56
  373.1 139.6 %copy-start.1 = (f32[256,320]{0,1:T(8,128)S(1)}, f32[256,320]{0,1:T(8,128)}, u32[]{:S(2)}) copy-start(f32[256,320]{0,1:T(8,128)} %all-reduce.8.cloned.1.call-done) | copy-start | bytes 983044
  373.1 270.9 %all-reduce.12.cloned.1.call-start = ((), (), s32[]{:S(2)}) async-start(), calls=%async_computation.3 | async-start | bytes 1638400 | tf_op jit(solution)/shard_map/psum | solution.py:61
  513.7 0.7 copy-start.8
  515.7 128.3 %copy-start.2 = (f32[256,800]{0,1:T(8,128)S(1)}, f32[256,800]{0,1:T(8,128)}, u32[]{:S(2)}) copy-start(f32[256,800]{0,1:T(8,128)} %get-tuple-element.7) | copy-start | bytes 2457604
  515.7 128.3 %copy-start.3 = (f32[256,800]{0,1:T(8,128)S(1)}, f32[256,800]{0,1:T(8,128)}, u32[]{:S(2)}) copy-start(f32[256,800]{0,1:T(8,128)} %get-tuple-element.8) | copy-start | bytes 2457604
  515.8 271.1 %all-reduce.14.cloned.1.call-start = ((), (), s32[]{:S(2)}) async-start(), calls=%async_computation.4 | async-start | bytes 655360 | tf_op jit(solution)/shard_map/psum | solution.py:79
  644.0 1.6 copy-start.5
  645.6 1.5 copy-start.7
  648.2 165.2 %copy-start.9 = (f32[256,320]{0,1:T(8,128)S(1)}, f32[256,320]{0,1:T(8,128)}, u32[]{:S(2)}) copy-start(f32[256,320]{0,1:T(8,128)} %all-reduce.10.cloned.1.call-done) | copy-start | bytes 983044
  649.4 165.1 %copy-start.11 = (bf16[256,160]{1,0:T(8,128)(2,1)S(1)}, bf16[256,160]{1,0:T(8,128)(2,1)}, u32[]{:S(2)}) copy-start(bf16[256,160]{1,0:T(8,128)(2,1)} %copy-done.10) | copy-start | bytes 245764
  788.6 26.2 %copy-start.13 = (bf16[256,160]{1,0:T(8,128)(2,1)S(1)}, bf16[256,160]{1,0:T(8,128)(2,1)}, u32[]{:S(2)}) copy-start(bf16[256,160]{1,0:T(8,128)(2,1)} %copy-done.12) | copy-start | bytes 245764
Sparse Core Ops, SparseCore 0:
  60.8 143.5 all-reduce.7
  234.1 136.2 all-reduce.15
  374.5 138.0 all-reduce.9
  515.9 128.0 all-reduce.11
  648.4 138.4 all-reduce.13
where the time goes:
time: 828 us; the launch traced here: 822 us
  waiting for transfers between devices  651 us (79%)
  blocking collectives  119 us (14%)
  matrix products  14.8 us (2%)
  between operations  14.6 us (2%)
  other arithmetic  10.2 us (1%)
    psum x1, waiting for transfers between devices, shards(): mixed_in = lax.psum(fc_part, 'fsdp')  144 us
    psum x1, waiting for transfers between devices, shards(): lax.psum(jnp.dot(activated, down_weight, preferred_element_type=jnp.float...  139 us
    psum x1, waiting for transfers between devices, shards(): back_norm = lax.psum(norm_terms, 'fsdp')  137 us
    psum x1, waiting for transfers between devices, shards(): lax.psum(jnp.einsum('rd,fd->rf', loss_grad_b, down_weight, preferred_elem...  126 us
    psum x1, waiting for transfers between devices, shards(): lax.psum((jnp.dot(normed, gate_weight, preferred_element_type=jnp.float32...  105 us
    all_gather x1, blocking collectives, shards(): lax.all_gather(embed_rows, 'roll', axis=0, tiled=True)  30.2 us
    psum x1, blocking collectives, shards(): inner = lax.psum(jnp.sum(gained * mixed_in, axis=1), 'roll')[:, None] / D  24.8 us
    psum x1, blocking collectives, shards(): squares = lax.psum(jnp.sum(mixed_in * mixed_in, axis=1), 'roll')  24.7 us
  transfers between devices with their start and end apart: 6, of which 5 were waited for; matrix products, arithmetic and copies ran while one was open for 1% of the time, Pallas kernels for 0%

commit v1 on v0

v1 whole, which is shorter than its diff:
```python
import math

import jax
import jax.numpy as jnp
from jax import lax
from jax.experimental import pallas as pl
from jax.experimental.pallas import tpu as pltpu
from jax.sharding import PartitionSpec as P

D = 5120
ROWS = 128
CAP = 16
NZ = 16
NF = 32
DB = 320
DP = 384
FB = 800
FP = 896
PIECE = DB // NF
META = 832
EPS = 1e-06
SCALE = 1.0 / math.sqrt(ROWS)
F32 = jnp.float32
BF16 = jnp.bfloat16
MESH = pl.DeviceIdType.MESH


def dot(a, b, ca=1, cb=0):
    return lax.dot_general(a, b, (((ca,), (cb,)), ((), ())), preferred_element_type=F32)


def iota(shape, axis):
    return lax.broadcasted_iota(jnp.int32, shape, axis)


def pack_into(ref, tiles):
    low = iota((ROWS, 128), 0) % 8 < 4
    k0, k1, k2, k3 = tiles
    down = [pltpu.roll(t, 4, 0) for t in (k1, k3)]
    up = [pltpu.roll(t, ROWS - 4, 0) for t in (k0, k2)]
    even = [jnp.where(low, k0, down[0]), jnp.where(low, k2, down[1])]
    odd = [jnp.where(low, up[0], k1), jnp.where(low, up[1], k3)]
    halves = [jnp.concatenate([t.reshape(16, 8, 128) for t in pair], axis=1) for pair in (even, odd)]
    ref[...] = jnp.stack(halves, axis=1).reshape(NF, 16, 128).astype(ref.dtype)


def unpack(packed):
    packed = packed.reshape(16, 2, 16, 128)
    low = iota((ROWS, 128), 0) % 8 < 4
    e0 = packed[:, 0, 0:8].reshape(ROWS, 128)
    e1 = packed[:, 0, 8:16].reshape(ROWS, 128)
    o0 = packed[:, 1, 0:8].reshape(ROWS, 128)
    o1 = packed[:, 1, 8:16].reshape(ROWS, 128)
    down = [pltpu.roll(t, 4, 0) for t in (o0, o1)]
    up = [pltpu.roll(t, ROWS - 4, 0) for t in (e0, e1)]
    return (
        jnp.where(low, e0, down[0]),
        jnp.where(low, up[0], o0),
        jnp.where(low, e1, down[1]),
        jnp.where(low, up[1], o1),
    )


def split(x):
    high = x.astype(BF16).astype(F32)
    return high, x - high


def fold(x):
    n = x.shape[0] // 8
    tail = jnp.concatenate([x[:, 512:], jnp.zeros((n * 8, 128), x.dtype)], axis=1)
    return jnp.concatenate([x[:, :512].reshape(n, 8, 512), tail.reshape(n, 8, 512)], axis=1)


def unfold(x):
    n = x.shape[0]
    head = x[:, 0:8].reshape(n * 8, 512)
    tail = x[:, 8:16, 0:384].reshape(n * 8, 384)
    return jnp.concatenate([head, tail], axis=1)


def kernel(
    counts_ref,
    hidden_ref,
    embed_ref,
    target_ref,
    gain_ref,
    fc_hbm,
    gate_hbm,
    up_hbm,
    down_hbm,
    grad_fc_ref,
    grad_gain_ref,
    grad_gate_ref,
    grad_up_ref,
    grad_down_ref,
    fc_v,
    gate_v,
    up_v,
    down_v,
    fc_w,
    gate_w,
    up_w,
    down_w,
    a_src,
    a_dst,
    b1_src,
    b1_dst,
    b2_buf,
    d1_src,
    d1_dst,
    d2_buf,
    e1_src,
    e1_dst,
    e2_buf,
    f1_src,
    f1_dst,
    f2_buf,
    g1_src,
    g1_dst,
    g2_buf,
    load_sem,
    send_sem,
    recv_sem,
):
    z = lax.axis_index("roll")
    f = lax.axis_index("fsdp")

    def z_peer(i):
        offset = 8 + (i + 1) // 2 * (1 - 2 * (i % 2))
        return lax.rem(z + offset, NZ)

    def f_peer(i):
        return lax.rem(f + 1 + i, NF)

    loads = [
        pltpu.make_async_copy(a, b, load_sem.at[i])
        for i, (a, b) in enumerate(
            ((fc_hbm, fc_v), (gate_hbm, gate_v), (up_hbm, up_v), (down_hbm, down_v))
        )
    ]
    for load in loads:
        load.start()

    barrier = pltpu.get_barrier_semaphore()

    def greet_z(i, c):
        pl.semaphore_signal(barrier, inc=1, device_id=(z_peer(i), f), device_id_type=MESH)
        return c

    def greet_f(i, c):
        pl.semaphore_signal(barrier, inc=1, device_id=(z, f_peer(i)), device_id_type=MESH)
        return c

    lax.fori_loop(0, NZ - 1, greet_z, 0)
    lax.fori_loop(0, NF - 1, greet_f, 0)

    def send_z(phase, src, dst):
        def step(i, c):
            p = z_peer(i)
            pltpu.make_async_remote_copy(
                src_ref=dst.at[z] if src is None else src.at[p],
                dst_ref=dst.at[z],
                send_sem=send_sem.at[phase],
                recv_sem=recv_sem.at[phase],
                device_id=(p, f),
                device_id_type=MESH,
            ).start()
            return c

        lax.fori_loop(0, NZ - 1, step, 0)

    def send_f(phase, src, dst):
        def step(i, c):
            p = f_peer(i)
            pltpu.make_async_remote_copy(
                src_ref=dst.at[f] if src is None else src.at[p],
                dst_ref=dst.at[f],
                send_sem=send_sem.at[phase],
                recv_sem=recv_sem.at[phase],
                device_id=(z, p),
                device_id_type=MESH,
            ).start()
            return c

        lax.fori_loop(0, NF - 1, step, 0)

    def wait_z(sem, buf):
        part = buf.at[pl.ds(0, NZ - 1)]
        pltpu.make_async_copy(part, part, sem).wait()

    def wait_f(sem, buf):
        part = buf.at[pl.ds(0, NF - 1)]
        pltpu.make_async_copy(part, part, sem).wait()

    col = iota((160, DP), 1)
    row = iota((160, DP), 0)
    base = dot(embed_ref[...], (col == row).astype(F32).astype(BF16)) + dot(
        hidden_ref[...], (col == row + 160).astype(F32).astype(BF16)
    )
    base = jnp.where(iota((CAP, DP), 1) == DP - 1, counts_ref[0].astype(F32), base)
    wide = jnp.concatenate([target_ref[:, 640 * p : 640 * p + 640] for p in range(8)], axis=0)
    col = iota((640, 256), 1)
    row = iota((640, 256), 0)
    lane = col % 128 - 64
    wanted = row == col // 128 * DB + PIECE * f + lane
    pick = jnp.where((lane >= 0) & (lane < PIECE) & wanted, 1.0, 0.0).astype(BF16)
    pieces = dot(wide, pick)
    for p in range(NZ):
        piece = pieces[p // 2 * 16 : p // 2 * 16 + 16, p % 2 * 128 : p % 2 * 128 + 128]
        a_src[p, :, 0:256] = base[:, 0:256].astype(BF16)
        a_src[p, :, 256:384] = (base[:, 256:384] + piece).astype(BF16)
    a_dst[pl.ds(z, 1)] = a_src[pl.ds(z, 1)]

    pl.semaphore_wait(barrier, NZ - 1 + NF - 1)
    send_z(0, a_src, a_dst)

    fc_w[...] = jnp.zeros_like(fc_w)
    gate_w[...] = jnp.zeros_like(gate_w)
    up_w[...] = jnp.zeros_like(up_w)
    down_w[...] = jnp.zeros_like(down_w)
    for load in loads:
        load.wait()
    fc_w[0:DB, 0:DB] = fc_v[...]
    gate_w[0:DB, 0:FB] = gate_v[...]
    up_w[0:DB, 0:FB] = up_v[...]
    down_w[0:FB, 0:DB] = down_v[...]
    gain = jnp.concatenate(
        [gain_ref[:, 0:256], jnp.concatenate([gain_ref[:, 256:320], jnp.ones((1, 64), F32)], axis=1)],
        axis=1,
    )
    packed_row = iota((16, 128), 0)
    gain_p = jnp.where(
        packed_row < 4,
        gain[:, 0:128],
        jnp.where(packed_row < 8, gain[:, 128:256], gain[:, 256:384]),
    )
    wait_z(recv_sem.at[0], a_dst)

    slots = a_dst[...].reshape(NZ * CAP, DP)
    before = jnp.where(iota((256, 256), 1) // CAP < iota((256, 256), 0) // CAP, 1.0, 0.0).astype(BF16)
    start = dot(before, slots[:, 256:384])[:, 127:128] * (1.0 / CAP)
    count = slots[:, 256:384].astype(F32)[:, 127:128]
    place = (iota((256, ROWS), 0) % CAP).astype(F32)
    goes = iota((256, ROWS), 1).astype(F32) == start + place
    select = jnp.where((place < count) & goes, 1.0, 0.0).astype(BF16)
    live = dot(select, slots, 0, 0).astype(BF16)
    fc_part = dot(live, fc_w[...])
    none = jnp.zeros((ROWS, 128), F32)
    pack_into(b1_src, (fc_part[:, 0:128], fc_part[:, 128:256], fc_part[:, 256:384], none))
    mine_f = pl.ds(f, 1)
    b1_dst[mine_f] = b1_src[mine_f]
    send_f(1, b1_src, b1_dst)
    col = iota((128, DP), 1)
    row = iota((128, DP), 0) - 64
    lay = jnp.where((row >= 0) & (row < PIECE) & (col == PIECE * f + row), 1.0, 0.0).astype(BF16)
    target_part = dot(live[:, 256:384], lay)
    wait_f(recv_sem.at[1], b1_dst)

    def total_f(buf):
        return jnp.sum(buf[...].astype(F32), axis=0)

    mixed = total_f(b1_dst)
    b2_buf[mine_f] = (mixed * gain_p).astype(BF16).reshape(1, 16, 128)
    send_f(2, None, b2_buf)
    wait_f(recv_sem.at[2], b2_buf)

    h_tiles = unpack(b2_buf[...].astype(F32))
    h = jnp.concatenate(h_tiles[:3], axis=1)
    plain = h / gain
    squares = jnp.sum(plain * plain, axis=1, keepdims=True)
    h = h.astype(BF16)
    gate_part = dot(h, gate_w[...])
    up_part = dot(h, up_w[...])
    sq_high, sq_low = split(squares)
    lane = iota((ROWS, FP), 1)
    gate_part = jnp.where(lane == META, sq_high, jnp.where(lane == META + 1, sq_low, gate_part))
    d1_src[...] = jnp.concatenate(
        [gate_part.reshape(NZ, 8, FP), up_part.reshape(NZ, 8, FP)], axis=1
    ).astype(BF16)
    mine_z = pl.ds(z, 1)
    d1_dst[mine_z] = d1_src[mine_z]
    send_z(3, d1_src, d1_dst)
    wait_z(recv_sem.at[3], d1_dst)

    both = jnp.sum(d1_dst[...].astype(F32), axis=0)
    gate_sum, up_sum = both[0:8], both[8:16]
    lane8 = iota((8, FP), 1)
    square = jnp.sum(
        jnp.where((lane8 == META) | (lane8 == META + 1), gate_sum, 0.0), axis=1, keepdims=True
    )
    inverse = lax.rsqrt(square / D + EPS)
    real = lane8 < FB
    gate_pre = jnp.where(real, gate_sum * inverse, 0.0)
    up_pre = up_sum * inverse
    sig = jax.nn.sigmoid(gate_pre)
    act = gate_pre * sig * up_pre
    d2_buf[mine_z] = fold(act).astype(BF16)
    send_z(4, None, d2_buf)
    wait_z(recv_sem.at[4], d2_buf)

    act_all = unfold(d2_buf[...].astype(F32)).astype(BF16)
    down_part = dot(act_all, down_w[...]) - target_part
    pack_into(e1_src, (down_part[:, 0:128], down_part[:, 128:256], down_part[:, 256:384], none))
    e1_dst[mine_f] = e1_src[mine_f]
    send_f(5, e1_src, e1_dst)
    wait_f(recv_sem.at[5], e1_dst)

    loss_grad = (mixed + total_f(e1_dst)) * SCALE
    e2_buf[mine_f] = loss_grad.astype(BF16).reshape(1, 16, 128)
    send_f(6, None, e2_buf)
    wait_f(recv_sem.at[6], e2_buf)

    loss_all = jnp.concatenate(unpack(e2_buf[...].astype(F32))[:3], axis=1).astype(BF16)
    back_part = dot(loss_all, down_w[...], 1, 1)
    f1_src[...] = fold(back_part).astype(BF16)
    f1_dst[mine_z] = f1_src[mine_z]
    send_z(7, f1_src, f1_dst)
    grad_down_ref[...] = dot(act_all, loss_all, 0, 0)[0:FB, 0:DB]
    wait_z(recv_sem.at[7], f1_dst)

    back_act = unfold(jnp.sum(f1_dst[...].astype(F32), axis=0, keepdims=True))
    back_gate = back_act * up_pre * sig * (1.0 + gate_pre * (1.0 - sig))
    back_up = back_act * gate_pre * sig
    inner = inverse * inverse / D * jnp.sum(
        jnp.where(real, back_gate * gate_pre + back_up * up_pre, 0.0), axis=1, keepdims=True
    )
    in_high, in_low = split(inner)
    back_gate = jnp.where(real, back_gate * inverse, 0.0)
    back_gate = jnp.where(lane8 == META, in_high, jnp.where(lane8 == META + 1, in_low, back_gate))
    back_up = jnp.where(real, back_up * inverse, 0.0)
    f2_buf[mine_z] = jnp.concatenate([back_gate, back_up], axis=0).astype(BF16).reshape(1, 16, FP)
    send_z(8, None, f2_buf)
    wait_z(recv_sem.at[8], f2_buf)

    back_both = f2_buf[...].astype(F32)
    bg_all = back_both[:, 0:8].reshape(ROWS, FP)
    bu_all = back_both[:, 8:16].reshape(ROWS, FP).astype(BF16)
    lane = iota((ROWS, 128), 1) + 768
    inner_tile = jnp.where((lane == META) | (lane == META + 1), bg_all[:, 768:896], 0.0)
    bg_all = bg_all.astype(BF16)
    norm_part = dot(bg_all, gate_w[...], 1, 1) + dot(bu_all, up_w[...], 1, 1)
    pack_into(g1_src, (norm_part[:, 0:128], norm_part[:, 128:256], norm_part[:, 256:384], inner_tile))
    g1_dst[mine_f] = g1_src[mine_f]
    send_f(9, g1_src, g1_dst)
    grad_gate_ref[...] = dot(h, bg_all, 0, 0)[0:DB, 0:FB].astype(BF16)
    grad_up_ref[...] = dot(h, bu_all, 0, 0)[0:DB, 0:FB].astype(BF16)
    wait_f(recv_sem.at[9], g1_dst)

    back_norm = total_f(g1_dst)
    inner_col = jnp.sum(jnp.where(packed_row >= 12, back_norm, 0.0), axis=1, keepdims=True)
    inner_col = jnp.broadcast_to(inner_col, (16, 128))
    inner_all = pltpu.roll(inner_col, 4, 0) + pltpu.roll(inner_col, 8, 0) + pltpu.roll(inner_col, 12, 0)
    back_mix = loss_grad + gain_p * back_norm - mixed * inner_all
    terms = back_norm * mixed
    gain_sums = [
        jnp.sum(jnp.where(packed_row // 4 == k, terms, 0.0), axis=0, keepdims=True) for k in range(3)
    ]
    for k in range(3):
        back_mix = jnp.where(packed_row == 12 + k, gain_sums[k], back_mix)
    g2_buf[mine_f] = back_mix.astype(BF16).reshape(1, 16, 128)
    send_f(10, None, g2_buf)
    wait_f(recv_sem.at[10], g2_buf)

    mix_packed = g2_buf[...].astype(F32)
    mix_all = jnp.concatenate(unpack(mix_packed)[:3], axis=1).astype(BF16)
    grad_fc_ref[...] = dot(live, mix_all, 0, 0)[0:DB, 0:DB]
    gain_total = jnp.sum(mix_packed, axis=0)
    for k in range(3):
        grad_gain_ref[:, 128 * k : 128 * k + 128] = gain_total[12 + k : 13 + k]

    for phase, buf in ((0, a_dst), (3, d1_dst), (4, d2_buf), (7, f1_dst), (8, f2_buf)):
        wait_z(send_sem.at[phase], buf)
    for phase, buf in ((1, b1_dst), (2, b2_buf), (5, e1_dst), (6, e2_buf), (9, g1_dst), (10, g2_buf)):
        wait_f(send_sem.at[phase], buf)


def shards(
    hidden_rows,
    embed_rows,
    target_rows,
    counts,
    fc_weight,
    norm_gain,
    gate_weight,
    up_weight,
    down_weight,
):
    vmem = pl.BlockSpec(memory_space=pltpu.VMEM)
    hbm = pl.BlockSpec(memory_space=pl.ANY)
    xy = pltpu.VMEM((NF, 16, 128), BF16)
    grad_fc, grad_gain, grad_gate, grad_up, grad_down = pl.pallas_call(
        kernel,
        out_shape=(
            jax.ShapeDtypeStruct((DB, DB), F32),
            jax.ShapeDtypeStruct((1, DP), F32),
            jax.ShapeDtypeStruct((DB, FB), BF16),
            jax.ShapeDtypeStruct((DB, FB), BF16),
            jax.ShapeDtypeStruct((FB, DB), F32),
        ),
        in_specs=[pl.BlockSpec(memory_space=pltpu.SMEM)] + [vmem] * 4 + [hbm] * 4,
        out_specs=[vmem] * 5,
        scratch_shapes=[
            pltpu.VMEM((DB, DB), BF16),
            pltpu.VMEM((DB, FB), BF16),
            pltpu.VMEM((DB, FB), BF16),
            pltpu.VMEM((FB, DB), BF16),
            pltpu.VMEM((DP, DP), BF16),
            pltpu.VMEM((DP, FP), BF16),
            pltpu.VMEM((DP, FP), BF16),
            pltpu.VMEM((FP, DP), BF16),
            pltpu.VMEM((NZ, CAP, DP), BF16),
            pltpu.VMEM((NZ, CAP, DP), BF16),
            xy,
            xy,
            xy,
            pltpu.VMEM((NZ, 16, FP), BF16),
            pltpu.VMEM((NZ, 16, FP), BF16),
            pltpu.VMEM((NZ, 16, 512), BF16),
            xy,
            xy,
            xy,
            pltpu.VMEM((NZ, 16, 512), BF16),
            pltpu.VMEM((NZ, 16, 512), BF16),
            pltpu.VMEM((NZ, 16, FP), BF16),
            xy,
            xy,
            xy,
            pltpu.SemaphoreType.DMA((4,)),
            pltpu.SemaphoreType.DMA((11,)),
            pltpu.SemaphoreType.DMA((11,)),
        ],
        compiler_params=pltpu.CompilerParams(
            collective_id=0, has_side_effects=True, vmem_limit_bytes=48 << 20
        ),
        name="draft_layer",
    )(
        counts,
        hidden_rows,
        embed_rows,
        target_rows,
        norm_gain.reshape(1, DB),
        fc_weight.reshape(DB, DB),
        gate_weight,
        up_weight,
        down_weight,
    )
    return (
        grad_fc.reshape(2, DB // 2, DB),
        grad_gain[0, :DB],
        grad_gate,
        grad_up,
        grad_down,
    )


def solution(mesh):
    placed = (
        P("roll", "fsdp"),
        P("roll", "fsdp"),
        P("roll", None),
        P("roll"),
        P(None, "fsdp", "roll"),
        P("roll"),
        P("roll", "fsdp"),
        P("roll", "fsdp"),
        P("fsdp", "roll"),
    )
    return jax.shard_map(
        shards,
        mesh=mesh,
        in_specs=placed,
        out_specs=(
            P(None, "fsdp", "roll"),
            P("roll"),
            P("roll", "fsdp"),
            P("roll", "fsdp"),
            P("fsdp", "roll"),
        ),
        check_vma=False,
    )
```

time: 828 us -> 148 us (0.18)
  waiting for transfers between devices: 651 us -> 0 us
  Pallas kernels: 0 us -> 135 us
  blocking collectives: 119 us -> 0 us
  matrix products: 14.8 us -> 0 us
  between operations: 14.6 us -> 1.35 us
  other arithmetic: 10.2 us -> 0 us
    psum x5 -> x0, waiting for transfers between devices: 651 us -> none  [the longest x1 144 us: shards(): mixed_in = lax.psum(fc_part, 'fsdp')]
    pallas_call x0 -> x1, Pallas kernels: none -> 135 us  [shards(): pl.pallas_call(kernel, out_shape=(jax.ShapeDtypeStruct((DB, DB), F32), ja...]
    all_gather x2 -> x0, blocking collectives: 50.3 us -> none  [the longest x1 30.2 us: shards(): lax.all_gather(embed_rows, 'roll', axis=0, tiled=True)]
    psum x2 -> x0, blocking collectives: 49.5 us -> none  [the longest x1 24.8 us: shards(): inner = lax.psum(jnp.sum(gained * mixed_in, axis=1), 'roll')[:, None] / D]
    unnamed x1 -> x0, blocking collectives: 19.2 us -> none
    dot_general x13 -> x0, matrix products: 14.8 us -> none  [the longest x1 2.39 us: shards(): jnp.einsum('rf,rd->fd', activated, loss_grad_b, preferred_element_type=jn...]
  transfers between devices with their start and end apart: 6 -> 0, of which waited for: 5 -> 0; matrix products, arithmetic and copies ran while one was open for 1% -> 0% of each run, Pallas kernels for 0% -> 0%
where the time goes in v1:
time: 148 us
  Pallas kernels  135 us (91%)
  local copies, waits for them, and re-layouts  11.4 us (8%)
    pallas_call x1, Pallas kernels, shards(): pl.pallas_call(kernel, out_shape=(jax.ShapeDtypeStruct((DB, DB), F32), ja...  135 us
    unnamed x25, local copies, waits for them, and re-layouts  10.2 us

profile of v1, /device:TPU:1, one launch (start us, length us, event | category | flops | bytes accessed | tf_op | source)
XLA Modules:
  0.0 147.7 jit_solution(8132439746620885150)
XLA Ops:
  0.6 0.0 copy-start
  0.6 0.0 copy-start.1
  0.7 1.5 copy.14.down_hbm
  2.1 0.7 reshape.19.gain_ref
  3.5 0.0 copy-done
  3.5 0.0 copy-done.1
  3.5 0.0 copy-start.6
  3.5 0.9 copy-done.6
  4.4 0.0 copy-start.7
  4.4 0.9 copy-done.7
  5.3 0.0 copy-start.8
  5.3 0.7 copy-done.8
  6.0 0.0 copy-start.9
  6.0 0.7 copy-done.9
  6.7 134.9 %draft_layer.1 = (f32[320,320]{1,0:T(8,128)S(1)}, f32[1,384]{1,0:T(1,128)S(1)}, bf16[320,800]{1,0:T(8,128)(2,1)S(1)}, bf16[320,800]{1,0:T(8,128)(2,1)S(1)}, f32[800,320]{1,0:T(8,128)S(1)}) custom-call(s32[1]{0:T(128)S(6)} %copy.19.counts_ref, bf16[16,160]{1,0:T(8,128)(2,1)S(1)} %copy-done.8, bf16[16,160]{1,0:T(8,128)(2,1)S(1)} %copy-done.9, ...), custom_call_target="tpu_custom_call" | custom-call | tf_op jit(solution)/shard_map/draft_layer/pallas_call | solution.py:392
  141.6 0.0 copy-start.2
  141.6 0.8 copy-done.2
  142.4 0.0 copy-start.4
  142.4 0.8 copy-done.4
  143.2 0.0 copy-start.5
  143.2 1.4 copy.15
  144.7 0.0 copy-start.3
  144.7 0.6 slice_reduce_fusion
  145.2 0.8 copy.20
  146.0 0.0 copy-done.5
  146.0 0.8 copy.21
  146.8 0.0 copy-done.3
  146.8 0.8 copy.22
Async XLA Ops:
  0.6 2.8 %copy-start = (bf16[320,800]{1,0:T(8,128)(2,1)S(1)}, bf16[320,800]{1,0:T(8,128)(2,1)}, u32[]{:S(2)}) copy-start(bf16[320,800]{1,0:T(8,128)(2,1)} %gate_hbm.1) | copy-start | bytes 1536004
  0.6 2.8 %copy-start.1 = (bf16[320,800]{1,0:T(8,128)(2,1)S(1)}, bf16[320,800]{1,0:T(8,128)(2,1)}, u32[]{:S(2)}) copy-start(bf16[320,800]{1,0:T(8,128)(2,1)} %up_hbm.1) | copy-start | bytes 1536004
  3.5 0.9 copy-start.6
  4.4 0.9 copy-start.7
  5.3 0.7 copy-start.8
  6.0 0.7 copy-start.9
  141.6 0.8 copy-start.2
  142.4 0.8 copy-start.4
  143.2 2.8 %copy-start.5 = (bf16[320,800]{1,0:T(8,128)(2,1)S(1)}, bf16[320,800]{1,0:T(8,128)(2,1)}, u32[]{:S(2)}) copy-start(bf16[320,800]{1,0:T(8,128)(2,1)} %copy-done.4) | copy-start | bytes 1536004
  144.7 2.2 %copy-start.3 = (bf16[320,800]{1,0:T(8,128)(2,1)S(1)}, bf16[320,800]{1,0:T(8,128)(2,1)}, u32[]{:S(2)}) copy-start(bf16[320,800]{1,0:T(8,128)(2,1)} %copy-done.2) | copy-start | bytes 1536004

commit v2 on v1

v2 whole, which is shorter than its diff:
```python
import math

import jax
import jax.numpy as jnp
from jax import lax
from jax.experimental import pallas as pl
from jax.experimental.pallas import tpu as pltpu
from jax.sharding import PartitionSpec as P

D = 5120
ROWS = 128
CAP = 16
NZ = 16
NF = 32
DB = 320
DP = 384
FB = 800
FP = 896
PIECE = DB // NF
META = 832
EPS = 1e-06
SCALE = 1.0 / math.sqrt(ROWS)
F32 = jnp.float32
BF16 = jnp.bfloat16
MESH = pl.DeviceIdType.MESH
Z_PEERS = (8, 4, -4, 3, -3, 2, -2, 1, -1)


def dot(a, b, ca=1, cb=0):
    return lax.dot_general(a, b, (((ca,), (cb,)), ((), ())), preferred_element_type=F32)


def iota(shape, axis):
    return lax.broadcasted_iota(jnp.int32, shape, axis)


def pack_into(ref, tiles):
    low = iota((ROWS, 128), 0) % 8 < 4
    k0, k1, k2, k3 = tiles
    down = [pltpu.roll(t, 4, 0) for t in (k1, k3)]
    up = [pltpu.roll(t, ROWS - 4, 0) for t in (k0, k2)]
    even = [jnp.where(low, k0, down[0]), jnp.where(low, k2, down[1])]
    odd = [jnp.where(low, up[0], k1), jnp.where(low, up[1], k3)]
    halves = [jnp.concatenate([t.reshape(16, 8, 128) for t in pair], axis=1) for pair in (even, odd)]
    ref[...] = jnp.stack(halves, axis=1).reshape(NF, 16, 128).astype(ref.dtype)


def unpack(packed):
    packed = packed.reshape(16, 2, 16, 128)
    low = iota((ROWS, 128), 0) % 8 < 4
    e0 = packed[:, 0, 0:8].reshape(ROWS, 128)
    e1 = packed[:, 0, 8:16].reshape(ROWS, 128)
    o0 = packed[:, 1, 0:8].reshape(ROWS, 128)
    o1 = packed[:, 1, 8:16].reshape(ROWS, 128)
    down = [pltpu.roll(t, 4, 0) for t in (o0, o1)]
    up = [pltpu.roll(t, ROWS - 4, 0) for t in (e0, e1)]
    return (
        jnp.where(low, e0, down[0]),
        jnp.where(low, up[0], o0),
        jnp.where(low, e1, down[1]),
        jnp.where(low, up[1], o1),
    )


def split(x):
    high = x.astype(BF16).astype(F32)
    return high, x - high


def fold(x):
    n = x.shape[0] // 8
    tail = jnp.concatenate([x[:, 512:], jnp.zeros((n * 8, 128), x.dtype)], axis=1)
    return jnp.concatenate([x[:, :512].reshape(n, 8, 512), tail.reshape(n, 8, 512)], axis=1)


def unfold(x):
    n = x.shape[0]
    head = x[:, 0:8].reshape(n * 8, 512)
    tail = x[:, 8:16, 0:384].reshape(n * 8, 384)
    return jnp.concatenate([head, tail], axis=1)


def seat(d):
    g = jnp.where(d == 0, 5, jnp.where(d == 1, 0, jnp.where(d == 15, 1, jnp.where(d == 2, 2, 3))))
    g = jnp.where(d == 8, 4, g)
    direct = 256 + 64 + PIECE * g
    up = 64 + PIECE * (d - 3)
    down = 128 + 64 + PIECE * (13 - d)
    return jnp.where((d >= 3) & (d <= 7), up, jnp.where((d >= 9) & (d <= 13), down, direct))


def kernel(
    counts_ref,
    hidden_hbm,
    embed_hbm,
    target_hbm,
    gain_hbm,
    fc_hbm,
    gate_hbm,
    up_hbm,
    down_hbm,
    grad_fc_ref,
    grad_gain_ref,
    grad_gate_ref,
    grad_up_ref,
    grad_down_ref,
    hidden_v,
    embed_v,
    target_v,
    gain_v,
    fc_v,
    gate_v,
    up_v,
    down_v,
    fc_w,
    gate_w,
    up_w,
    down_w,
    a_src,
    a_buf,
    b1_src,
    b1_dst,
    b2_buf,
    d1_src,
    d1_dst,
    d1_mid,
    d2_buf,
    e1_src,
    e1_dst,
    e2_buf,
    f1_src,
    f1_dst,
    f1_mid,
    f2_buf,
    g1_src,
    g1_dst,
    g2_buf,
    load_sem,
    send_sem,
    recv_sem,
):
    z = lax.axis_index("roll")
    f = lax.axis_index("fsdp")
    f_x, f_y, f_c = lax.div(f, 8), lax.rem(lax.div(f, 2), 4), lax.rem(f, 2)

    def z_at(offset):
        return lax.rem(z + (offset + NZ), NZ)

    def far_first(k):
        return lax.rem(10 - lax.div(k * (k + 1), 2), 4)

    def f_peer(i):
        j = lax.div(i, 2)
        x = lax.rem(f_x + far_first(lax.div(j, 4)), 4)
        y = lax.rem(f_y + far_first(lax.rem(j, 4)), 4)
        c = lax.rem(f_c + 1 + i, 2)
        return x * 8 + y * 2 + c

    loads = [
        pltpu.make_async_copy(a, b, load_sem.at[i])
        for i, (a, b) in enumerate(
            (
                (hidden_hbm, hidden_v),
                (embed_hbm, embed_v),
                (target_hbm, target_v),
                (gain_hbm, gain_v),
                (fc_hbm, fc_v),
                (gate_hbm, gate_v),
                (up_hbm, up_v),
                (down_hbm, down_v),
            )
        )
    ]
    for load in loads:
        load.start()

    barrier = pltpu.get_barrier_semaphore()

    def greet_f(i, c):
        pl.semaphore_signal(barrier, inc=1, device_id=(z, f_peer(i)), device_id_type=MESH)
        return c

    for d in Z_PEERS:
        pl.semaphore_signal(barrier, inc=1, device_id=(z_at(d), f), device_id_type=MESH)
    lax.fori_loop(0, NF - 1, greet_f, 0)

    def send_z(src, dst, d, phase, group):
        pltpu.make_async_remote_copy(
            src_ref=src,
            dst_ref=dst,
            send_sem=send_sem.at[phase],
            recv_sem=recv_sem.at[phase, group],
            device_id=(z_at(d), f),
            device_id_type=MESH,
        ).start()

    def settle(sem, buf, n):
        part = buf.at[pl.ds(0, n)]
        pltpu.make_async_copy(part, part, sem).wait()

    def gather_z(phase, buf, plus=None, minus=None):
        own = buf.at[z]
        send_z(own if plus is None else plus, own, 4, phase, 0)
        send_z(own if minus is None else minus, own, -4, phase, 1)
        for d in (8, 2, -2, 1, -1):
            send_z(own, own, d, phase, 2)

        def relay():
            settle(recv_sem.at[phase, 0], buf, 1)
            came = buf.at[z_at(-4)]
            for d in (3, 2, 1, -1):
                send_z(came, came, d, phase, 2)
            settle(recv_sem.at[phase, 1], buf, 1)
            came = buf.at[z_at(4)]
            for d in (-3, -2, -1, 1):
                send_z(came, came, d, phase, 2)

        return relay

    def wait_gather_z(phase, buf):
        settle(recv_sem.at[phase, 2], buf, 13)

    def reduce_z(phase, src, dst, mid):
        for at, d in ((3, 3), (2, 2), (1, 1), (0, -1)):
            send_z(src.at[z_at(d + 4)], dst.at[at], d, phase, 0)
            send_z(src.at[z_at(-d - 4)], dst.at[4 + at], -d, phase, 1)
        for at, d in ((10, 8), (11, 2), (12, -2), (13, 1), (14, -1)):
            send_z(src.at[z_at(d)], dst.at[at], d, phase, 2)
        for g, d in ((0, 4), (1, -4)):
            settle(recv_sem.at[phase, g], dst, 4)
            total = jnp.sum(dst[4 * g : 4 * g + 4].astype(F32), axis=0, keepdims=True)
            mid[g : g + 1] = (total + src[pl.ds(z_at(d), 1)].astype(F32)).astype(BF16)
            send_z(mid.at[g], dst.at[8 + g], d, phase, 2)

    def wait_reduce_z(phase, src, dst):
        settle(recv_sem.at[phase, 2], dst, 7)
        return jnp.sum(dst[8:15].astype(F32), axis=0) + src[pl.ds(z, 1)].astype(F32)[0]

    def send_f(phase, src, dst):
        def step(i, c):
            p = f_peer(i)
            pltpu.make_async_remote_copy(
                src_ref=dst.at[f] if src is None else src.at[p],
                dst_ref=dst.at[f],
                send_sem=send_sem.at[phase],
                recv_sem=recv_sem.at[phase, 0],
                device_id=(z, p),
                device_id_type=MESH,
            ).start()
            return c

        lax.fori_loop(0, NF - 1, step, 0)

    def wait_f(phase, buf):
        settle(recv_sem.at[phase, 0], buf, NF - 1)

    mine_z = pl.ds(z, 1)
    mine_f = pl.ds(f, 1)

    for load in loads[:4]:
        load.wait()
    col = iota((160, DP), 1)
    row = iota((160, DP), 0)
    base = dot(embed_v[...], (col == row).astype(F32).astype(BF16)) + dot(
        hidden_v[...], (col == row + 160).astype(F32).astype(BF16)
    )
    base = jnp.where(iota((CAP, DP), 1) == DP - 1, counts_ref[0].astype(F32), base)
    wide = jnp.concatenate([target_v[:, 640 * p : 640 * p + 640] for p in range(8)], axis=0)
    col = iota((640, 256), 1)
    row = iota((640, 256), 0)
    lane = col % 128
    wanted = row == col // 128 * DB + PIECE * f + lane
    pieces = dot(wide, jnp.where((lane < PIECE) & wanted, 1.0, 0.0).astype(BF16))
    line = [jnp.zeros((CAP, 128), F32), jnp.zeros((CAP, 128), F32)]
    for p in range(NZ):
        piece = pieces[p // 2 * 16 : p // 2 * 16 + 16, p % 2 * 128 : p % 2 * 128 + 128]
        shift = PIECE * p if p < 12 else PIECE * (p - 12)
        line[p // 12] += pltpu.roll(piece, shift, 1) if shift else piece
    line = jnp.concatenate(line, axis=1).astype(BF16)
    r = iota((256, 1), 0)
    r = jnp.where(r < 128, r, r - 8)
    receiver = (r * 205) >> 11
    goal = seat((receiver - z + NZ) % NZ) + r - receiver * PIECE
    goal = jnp.where(receiver < NZ, goal, -1)
    spread = jnp.where(goal == iota((256, 3 * 128), 1), 1.0, 0.0).astype(BF16)
    tails = dot(line, spread)
    for v in range(3):
        a_src[v, :, 0:256] = base[:, 0:256].astype(BF16)
        a_src[v, :, 256:384] = (base[:, 256:384] + tails[:, 128 * v : 128 * v + 128]).astype(BF16)
    a_buf[mine_z] = a_src[2:3]

    pl.semaphore_wait(barrier, len(Z_PEERS) + NF - 1)
    relay = gather_z(0, a_buf, a_src.at[0], a_src.at[1])

    fc_w[...] = jnp.zeros_like(fc_w)
    gate_w[...] = jnp.zeros_like(gate_w)
    up_w[...] = jnp.zeros_like(up_w)
    down_w[...] = jnp.zeros_like(down_w)
    for load in loads[4:]:
        load.wait()
    fc_w[0:DB, 0:DB] = fc_v[...]
    gate_w[0:DB, 0:FB] = gate_v[...]
    up_w[0:DB, 0:FB] = up_v[...]
    down_w[0:DB, 0:FB] = down_v[...]
    gain = gain_v[...].reshape(1, DB)
    gain = jnp.concatenate([gain, jnp.ones((1, DP - DB), F32)], axis=1)
    packed_row = iota((16, 128), 0)
    gain_p = jnp.where(
        packed_row < 4,
        gain[:, 0:128],
        jnp.where(packed_row < 8, gain[:, 128:256], gain[:, 256:384]),
    )
    relay()
    wait_gather_z(0, a_buf)

    slots = a_buf[...].reshape(NZ * CAP, DP)
    before = jnp.where(iota((256, 256), 1) // CAP < iota((256, 256), 0) // CAP, 1.0, 0.0).astype(BF16)
    start = dot(before, slots[:, 256:384])[:, 127:128] * (1.0 / CAP)
    count = slots[:, 256:384].astype(F32)[:, 127:128]
    place = (iota((256, ROWS), 0) % CAP).astype(F32)
    goes = iota((256, ROWS), 1).astype(F32) == start + place
    select = jnp.where((place < count) & goes, 1.0, 0.0).astype(BF16)
    group = seat((z - lax.div(iota((256, 1), 0), CAP) + NZ) % NZ) % 128
    lane = iota((256, 128), 1)
    meant = (lane >= group) & (lane < group + PIECE) | (lane < 64)
    tail = jnp.where(meant, slots[:, 256:384].astype(F32), 0.0).astype(BF16)
    slots = jnp.concatenate([slots[:, 0:256], tail], axis=1)
    live = dot(select, slots, 0, 0).astype(BF16)
    fc_part = dot(live, fc_w[...])
    none = jnp.zeros((ROWS, 128), F32)
    pack_into(b1_src, (fc_part[:, 0:128], fc_part[:, 128:256], fc_part[:, 256:384], none))
    b1_dst[mine_f] = b1_src[mine_f]
    send_f(1, b1_src, b1_dst)
    col = iota((128, DP), 1)
    row = iota((128, DP), 0) - 64
    inside = (row >= 0) & (row < 6 * PIECE)
    row = row - ((jnp.where(inside, row, 0) * 205) >> 11) * PIECE
    lay = jnp.where(inside & (col == PIECE * f + row), 1.0, 0.0).astype(BF16)
    target_part = dot(live[:, 256:384], lay)
    wait_f(1, b1_dst)

    def total_f(buf):
        return jnp.sum(buf[...].astype(F32), axis=0)

    mixed = total_f(b1_dst)
    b2_buf[mine_f] = (mixed * gain_p).astype(BF16).reshape(1, 16, 128)
    send_f(2, None, b2_buf)
    wait_f(2, b2_buf)

    h_tiles = unpack(b2_buf[...].astype(F32))
    h = jnp.concatenate(h_tiles[:3], axis=1)
    plain = h / gain
    squares = jnp.sum(plain * plain, axis=1, keepdims=True)
    h = h.astype(BF16)
    gate_part = dot(h, gate_w[...])
    up_part = dot(h, up_w[...])
    sq_high, sq_low = split(squares)
    lane = iota((ROWS, FP), 1)
    gate_part = jnp.where(lane == META, sq_high, jnp.where(lane == META + 1, sq_low, gate_part))
    d1_src[...] = jnp.concatenate(
        [gate_part.reshape(NZ, 8, FP), up_part.reshape(NZ, 8, FP)], axis=1
    ).astype(BF16)
    reduce_z(3, d1_src, d1_dst, d1_mid)
    both = wait_reduce_z(3, d1_src, d1_dst)
    gate_sum, up_sum = both[0:8], both[8:16]
    lane8 = iota((8, FP), 1)
    square = jnp.sum(
        jnp.where((lane8 == META) | (lane8 == META + 1), gate_sum, 0.0), axis=1, keepdims=True
    )
    inverse = lax.rsqrt(square / D + EPS)
    real = lane8 < FB
    gate_pre = jnp.where(real, gate_sum * inverse, 0.0)
    up_pre = up_sum * inverse
    sig = jax.nn.sigmoid(gate_pre)
    act = gate_pre * sig * up_pre
    d2_buf[mine_z] = fold(act).astype(BF16)
    gather_z(4, d2_buf)()
    wait_gather_z(4, d2_buf)

    act_all = unfold(d2_buf[...].astype(F32)).astype(BF16)
    down_part = dot(act_all, down_w[...], 1, 1) - target_part
    pack_into(e1_src, (down_part[:, 0:128], down_part[:, 128:256], down_part[:, 256:384], none))
    e1_dst[mine_f] = e1_src[mine_f]
    send_f(5, e1_src, e1_dst)
    wait_f(5, e1_dst)

    loss_grad = (mixed + total_f(e1_dst)) * SCALE
    e2_buf[mine_f] = loss_grad.astype(BF16).reshape(1, 16, 128)
    send_f(6, None, e2_buf)
    wait_f(6, e2_buf)

    loss_all = jnp.concatenate(unpack(e2_buf[...].astype(F32))[:3], axis=1).astype(BF16)
    back_part = dot(loss_all, down_w[...])
    f1_src[...] = fold(back_part).astype(BF16)
    reduce_z(7, f1_src, f1_dst, f1_mid)
    grad_down_ref[...] = dot(loss_all, act_all, 0, 0)[0:DB, 0:FB]
    back_act = wait_reduce_z(7, f1_src, f1_dst)
    back_act = unfold(back_act.reshape(1, 16, 512))
    back_gate = back_act * up_pre * sig * (1.0 + gate_pre * (1.0 - sig))
    back_up = back_act * gate_pre * sig
    inner = inverse * inverse / D * jnp.sum(
        jnp.where(real, back_gate * gate_pre + back_up * up_pre, 0.0), axis=1, keepdims=True
    )
    in_high, in_low = split(inner)
    back_gate = jnp.where(real, back_gate * inverse, 0.0)
    back_gate = jnp.where(lane8 == META, in_high, jnp.where(lane8 == META + 1, in_low, back_gate))
    back_up = jnp.where(real, back_up * inverse, 0.0)
    f2_buf[mine_z] = jnp.concatenate([back_gate, back_up], axis=0).astype(BF16).reshape(1, 16, FP)
    gather_z(8, f2_buf)()
    wait_gather_z(8, f2_buf)

    back_both = f2_buf[...].astype(F32)
    bg_all = back_both[:, 0:8].reshape(ROWS, FP)
    bu_all = back_both[:, 8:16].reshape(ROWS, FP).astype(BF16)
    lane = iota((ROWS, 128), 1) + 768
    inner_tile = jnp.where((lane == META) | (lane == META + 1), bg_all[:, 768:896], 0.0)
    bg_all = bg_all.astype(BF16)
    norm_part = dot(bg_all, gate_w[...], 1, 1) + dot(bu_all, up_w[...], 1, 1)
    pack_into(g1_src, (norm_part[:, 0:128], norm_part[:, 128:256], norm_part[:, 256:384], inner_tile))
    g1_dst[mine_f] = g1_src[mine_f]
    send_f(9, g1_src, g1_dst)
    grad_gate_ref[...] = dot(h, bg_all, 0, 0)[0:DB, 0:FB].astype(BF16)
    grad_up_ref[...] = dot(h, bu_all, 0, 0)[0:DB, 0:FB].astype(BF16)
    wait_f(9, g1_dst)

    back_norm = total_f(g1_dst)
    inner_col = jnp.sum(jnp.where(packed_row >= 12, back_norm, 0.0), axis=1, keepdims=True)
    inner_col = jnp.broadcast_to(inner_col, (16, 128))
    inner_all = pltpu.roll(inner_col, 4, 0) + pltpu.roll(inner_col, 8, 0) + pltpu.roll(inner_col, 12, 0)
    back_mix = loss_grad + gain_p * back_norm - mixed * inner_all
    terms = back_norm * mixed
    gain_sums = [
        jnp.sum(jnp.where(packed_row // 4 == k, terms, 0.0), axis=0, keepdims=True) for k in range(3)
    ]
    for k in range(3):
        back_mix = jnp.where(packed_row == 12 + k, gain_sums[k], back_mix)
    g2_buf[mine_f] = back_mix.astype(BF16).reshape(1, 16, 128)
    send_f(10, None, g2_buf)
    wait_f(10, g2_buf)

    mix_packed = g2_buf[...].astype(F32)
    mix_all = jnp.concatenate(unpack(mix_packed)[:3], axis=1).astype(BF16)
    grad_fc_ref[...] = dot(live, mix_all, 0, 0)[0:DB, 0:DB]
    gain_total = jnp.sum(mix_packed, axis=0)
    for k in range(3):
        grad_gain_ref[:, 128 * k : 128 * k + 128] = gain_total[12 + k : 13 + k]

    for phase, buf in ((0, a_buf), (3, d1_dst), (4, d2_buf), (7, f1_dst), (8, f2_buf)):
        settle(send_sem.at[phase], buf, NZ - 1)
    for phase, buf in ((1, b1_dst), (2, b2_buf), (5, e1_dst), (6, e2_buf), (9, g1_dst), (10, g2_buf)):
        settle(send_sem.at[phase], buf, NF - 1)


def store_kernel(*refs):
    sems = refs[10]
    copies = [pltpu.make_async_copy(refs[i], refs[5 + i], sems.at[i]) for i in range(5)]
    for copy in copies:
        copy.start()
    for copy in copies:
        copy.wait()


def shards(
    hidden_rows,
    embed_rows,
    target_rows,
    counts,
    fc_weight,
    norm_gain,
    gate_weight,
    up_weight,
    down_weight,
):
    vmem = pl.BlockSpec(memory_space=pltpu.VMEM)
    hbm = pl.BlockSpec(memory_space=pl.ANY)
    xy = pltpu.VMEM((NF, 16, 128), BF16)
    shapes = (
        jax.ShapeDtypeStruct((DB, DB), F32),
        jax.ShapeDtypeStruct((1, DP), F32),
        jax.ShapeDtypeStruct((DB, FB), BF16),
        jax.ShapeDtypeStruct((DB, FB), BF16),
        jax.ShapeDtypeStruct((DB, FB), F32),
    )
    found = pl.pallas_call(
        kernel,
        out_shape=shapes,
        in_specs=[pl.BlockSpec(memory_space=pltpu.SMEM)] + [hbm] * 8,
        out_specs=[vmem] * 5,
        scratch_shapes=[
            pltpu.VMEM((CAP, 160), BF16),
            pltpu.VMEM((CAP, 160), BF16),
            pltpu.VMEM((CAP, D), BF16),
            pltpu.VMEM((DB,), F32),
            pltpu.VMEM((DB, DB), BF16),
            pltpu.VMEM((DB, FB), BF16),
            pltpu.VMEM((DB, FB), BF16),
            pltpu.VMEM((DB, FB), BF16),
            pltpu.VMEM((DP, DP), BF16),
            pltpu.VMEM((DP, FP), BF16),
            pltpu.VMEM((DP, FP), BF16),
            pltpu.VMEM((DP, FP), BF16),
            pltpu.VMEM((3, CAP, DP), BF16),
            pltpu.VMEM((NZ, CAP, DP), BF16),
            xy,
            xy,
            xy,
            pltpu.VMEM((NZ, 16, FP), BF16),
            pltpu.VMEM((NZ - 1, 16, FP), BF16),
            pltpu.VMEM((2, 16, FP), BF16),
            pltpu.VMEM((NZ, 16, 512), BF16),
            xy,
            xy,
            xy,
            pltpu.VMEM((NZ, 16, 512), BF16),
            pltpu.VMEM((NZ - 1, 16, 512), BF16),
            pltpu.VMEM((2, 16, 512), BF16),
            pltpu.VMEM((NZ, 16, FP), BF16),
            xy,
            xy,
            xy,
            pltpu.SemaphoreType.DMA((8,)),
            pltpu.SemaphoreType.DMA((11,)),
            pltpu.SemaphoreType.DMA((11, 3)),
        ],
        compiler_params=pltpu.CompilerParams(
            collective_id=0, has_side_effects=True, vmem_limit_bytes=56 << 20
        ),
        name="draft_layer",
    )(
        counts,
        hidden_rows,
        embed_rows,
        target_rows,
        norm_gain,
        fc_weight.reshape(DB, DB),
        gate_weight,
        up_weight,
        down_weight.T,
    )
    grad_fc, grad_gain, grad_gate, grad_up, grad_down = pl.pallas_call(
        store_kernel,
        out_shape=shapes,
        in_specs=[vmem] * 5,
        out_specs=[hbm] * 5,
        scratch_shapes=[pltpu.SemaphoreType.DMA((5,))],
        name="store_results",
    )(*found)
    return (
        grad_fc.reshape(2, DB // 2, DB),
        grad_gain[0, :DB],
        grad_gate,
        grad_up,
        grad_down.T,
    )


def solution(mesh):
    placed = (
        P("roll", "fsdp"),
        P("roll", "fsdp"),
        P("roll", None),
        P("roll"),
        P(None, "fsdp", "roll"),
        P("roll"),
        P("roll", "fsdp"),
        P("roll", "fsdp"),
        P("fsdp", "roll"),
    )
    return jax.shard_map(
        shards,
        mesh=mesh,
        in_specs=placed,
        out_specs=(
            P(None, "fsdp", "roll"),
            P("roll"),
            P("roll", "fsdp"),
            P("roll", "fsdp"),
            P("fsdp", "roll"),
        ),
        check_vma=False,
    )
```

time: 148 us -> 116 us (0.78)
  Pallas kernels: 135 us -> 113 us
  local copies, waits for them, and re-layouts: 11.4 us -> 1.27 us
    pallas_call x1 -> x2, Pallas kernels: 135 us -> 113 us  [the longest x1 110 us: shards(): pl.pallas_call(kernel, out_shape=shapes, in_specs=[pl.BlockSpec(memory_sp...]
    unnamed x25 -> x0, local copies, waits for them, and re-layouts: 10.2 us -> none
where the time goes in v2:
time: 116 us
  Pallas kernels  113 us (97%)
  between operations  1.3 us (1%)
  local copies, waits for them, and re-layouts  1.27 us (1%)
    pallas_call x1, Pallas kernels, shards(): pl.pallas_call(kernel, out_shape=shapes, in_specs=[pl.BlockSpec(memory_sp...  110 us
    pallas_call x1, Pallas kernels, shards(): pl.pallas_call(store_kernel, out_shape=shapes, in_specs=[vmem] * 5, out_s...  3.35 us

profile of v2, /device:TPU:1, one launch (start us, length us, event | category | flops | bytes accessed | tf_op | source)
XLA Modules:
  0.0 115.8 jit_solution(6275121569104251435)
XLA Ops:
  1.3 109.9 %draft_layer.1 = (f32[320,320]{1,0:T(8,128)}, f32[1,384]{1,0:T(1,128)}, bf16[320,800]{1,0:T(8,128)(2,1)}, bf16[320,800]{1,0:T(8,128)(2,1)}, f32[320,800]{1,0:T(8,128)}) custom-call(s32[1]{0:T(128)S(6)} %copy.14.counts_ref, bf16[16,160]{1,0:T(8,128)(2,1)} %hidden_hbm.1, bf16[16,160]{1,0:T(8,128)(2,1)} %embed_hbm.1, bf16[16,5120]{1,0:T(8,128)(2,1)} %target_hbm.1, ...), custom_call_target="tpu_custom_call" | custom-call | tf_op jit(solution)/shard_map/draft_layer/pallas_call | solution.py:484
  111.2 3.4 %store_results.1 = (f32[320,320]{1,0:T(8,128)}, f32[1,384]{1,0:T(1,128)}, bf16[320,800]{1,0:T(8,128)(2,1)}, bf16[320,800]{1,0:T(8,128)(2,1)}, f32[320,800]{1,0:T(8,128)}) custom-call(f32[320,320]{1,0:T(8,128)} %get-tuple-element.15.refs_0_, f32[1,384]{1,0:T(1,128)} %get-tuple-element.16.refs_1_, bf16[320,800]{1,0:T(8,128)(2,1)} %get-tuple-element.17.refs_2_, ...), custom_call_target="tpu_custom_call" | custom-call | tf_op jit(solution)/shard_map/store_results/pallas_call | solution.py:540
  114.5 1.3 %slice_reduce_fusion = f32[320]{0:T(512)} fusion(f32[1,384]{1,0:T(1,128)} %get-tuple-element.21), kind=kLoop, calls=%fused_computation | loop fusion | bytes 2560 | tf_op jit(solution)/shard_map/slice | solution.py:550

commit v3 on v2

--- a/solution.py
+++ b/solution.py
@@ -17,13 +17,14 @@
 FB = 800
 FP = 896
 PIECE = DB // NF
+CUT = 384
 META = 832
 EPS = 1e-06
 SCALE = 1.0 / math.sqrt(ROWS)
 F32 = jnp.float32
 BF16 = jnp.bfloat16
 MESH = pl.DeviceIdType.MESH
-Z_PEERS = (8, 4, -4, 3, -3, 2, -2, 1, -1)
+Z_PEERS = (4, -4, 3, -3, 2, -2, 1, -1)
 
 
 def dot(a, b, ca=1, cb=0):
@@ -69,24 +70,31 @@
 
 def fold(x):
     n = x.shape[0] // 8
-    tail = jnp.concatenate([x[:, 512:], jnp.zeros((n * 8, 128), x.dtype)], axis=1)
-    return jnp.concatenate([x[:, :512].reshape(n, 8, 512), tail.reshape(n, 8, 512)], axis=1)
-
-
-def unfold(x):
+    tail = x[:, 256:]
+    if tail.shape[1] < 256:
+        tail = jnp.concatenate([tail, jnp.zeros((n * 8, 128), x.dtype)], axis=1)
+    return jnp.concatenate([x[:, :256].reshape(n, 8, 256), tail.reshape(n, 8, 256)], axis=1)
+
+
+def unfold(x, width):
     n = x.shape[0]
-    head = x[:, 0:8].reshape(n * 8, 512)
-    tail = x[:, 8:16, 0:384].reshape(n * 8, 384)
+    head = x[:, 0:8].reshape(n * 8, 256)
+    tail = x[:, 8:16, 0 : width - 256].reshape(n * 8, width - 256)
     return jnp.concatenate([head, tail], axis=1)
 
 
-def seat(d):
-    g = jnp.where(d == 0, 5, jnp.where(d == 1, 0, jnp.where(d == 15, 1, jnp.where(d == 2, 2, 3))))
-    g = jnp.where(d == 8, 4, g)
+def twin(x, y):
+    n, lanes = x.shape[0] // 8, x.shape[1]
+    return jnp.concatenate([x.reshape(n, 8, lanes), y.reshape(n, 8, lanes)], axis=1)
+
+
+def seat(d, side):
+    g = jnp.where(d == 0, 4, jnp.where(d == 1, 0, jnp.where(d == 15, 1, jnp.where(d == 2, 2, 3))))
     direct = 256 + 64 + PIECE * g
     up = 64 + PIECE * (d - 3)
     down = 128 + 64 + PIECE * (13 - d)
-    return jnp.where((d >= 3) & (d <= 7), up, jnp.where((d >= 9) & (d <= 13), down, direct))
+    rises = (d >= 3) & (d <= 7) | (d == 8) & (side > 0)
+    return jnp.where(rises, up, jnp.where((d >= 8) & (d <= 13), down, direct))
 
 
 def kernel(
@@ -99,11 +107,11 @@
     gate_hbm,
     up_hbm,
     down_hbm,
-    grad_fc_ref,
-    grad_gain_ref,
-    grad_gate_ref,
-    grad_up_ref,
-    grad_down_ref,
+    grad_fc_hbm,
+    grad_gain_hbm,
+    grad_gate_hbm,
+    grad_up_hbm,
+    grad_down_hbm,
     hidden_v,
     embed_v,
     target_v,
@@ -121,27 +129,43 @@
     b1_src,
     b1_dst,
     b2_buf,
-    d1_src,
-    d1_dst,
-    d1_mid,
-    d2_buf,
+    d1a_src,
+    d1a_dst,
+    d1a_mid,
+    d1b_src,
+    d1b_dst,
+    d1b_mid,
+    d2a_buf,
+    d2b_buf,
     e1_src,
     e1_dst,
     e2_buf,
-    f1_src,
-    f1_dst,
-    f1_mid,
-    f2_buf,
+    f1a_src,
+    f1a_dst,
+    f1a_mid,
+    f1b_src,
+    f1b_dst,
+    f1b_mid,
+    f2a_buf,
+    f2b_buf,
     g1_src,
     g1_dst,
     g2_buf,
+    grad_fc_v,
+    grad_gain_v,
+    grad_gate_v,
+    grad_up_v,
+    grad_down_v,
     load_sem,
+    out_sem,
     send_sem,
     recv_sem,
 ):
     z = lax.axis_index("roll")
     f = lax.axis_index("fsdp")
     f_x, f_y, f_c = lax.div(f, 8), lax.rem(lax.div(f, 2), 4), lax.rem(f, 2)
+
+    side = 1 - 2 * lax.rem(z, 2)
 
     def z_at(offset):
         return lax.rem(z + (offset + NZ), NZ)
@@ -198,43 +222,58 @@
         part = buf.at[pl.ds(0, n)]
         pltpu.make_async_copy(part, part, sem).wait()
 
-    def gather_z(phase, buf, plus=None, minus=None):
+    def gather_start(phase, buf, plus=None, minus=None):
         own = buf.at[z]
         send_z(own if plus is None else plus, own, 4, phase, 0)
         send_z(own if minus is None else minus, own, -4, phase, 1)
-        for d in (8, 2, -2, 1, -1):
+        for d in (2, -2, 1, -1):
             send_z(own, own, d, phase, 2)
 
-        def relay():
-            settle(recv_sem.at[phase, 0], buf, 1)
-            came = buf.at[z_at(-4)]
-            for d in (3, 2, 1, -1):
-                send_z(came, came, d, phase, 2)
-            settle(recv_sem.at[phase, 1], buf, 1)
-            came = buf.at[z_at(4)]
-            for d in (-3, -2, -1, 1):
-                send_z(came, came, d, phase, 2)
-
-        return relay
-
-    def wait_gather_z(phase, buf):
+    def gather_relay(phase, buf):
+        settle(recv_sem.at[phase, 0], buf, 1)
+        settle(recv_sem.at[phase, 1], buf, 1)
+        came = buf.at[z_at(-4 * side)]
+        send_z(came, came, 4 * side, phase, 2)
+        low, high = buf.at[z_at(-4)], buf.at[z_at(4)]
+        for d in (3, 2, 1, -1):
+            send_z(low, low, d, phase, 2)
+            send_z(high, high, -d, phase, 2)
+
+    def gather_end(phase, buf):
         settle(recv_sem.at[phase, 2], buf, 13)
 
-    def reduce_z(phase, src, dst, mid):
-        for at, d in ((3, 3), (2, 2), (1, 1), (0, -1)):
-            send_z(src.at[z_at(d + 4)], dst.at[at], d, phase, 0)
-            send_z(src.at[z_at(-d - 4)], dst.at[4 + at], -d, phase, 1)
-        for at, d in ((10, 8), (11, 2), (12, -2), (13, 1), (14, -1)):
-            send_z(src.at[z_at(d)], dst.at[at], d, phase, 2)
+    def reduce_start(phase, src, dst):
+        for own, d, slot, group in (
+            (8, -4 * side, 8, 3),
+            (7, 3, 3, 0),
+            (-7, -3, 7, 1),
+            (6, 2, 2, 0),
+            (-6, -2, 6, 1),
+            (5, 1, 1, 0),
+            (-5, -1, 5, 1),
+            (3, -1, 0, 0),
+            (-3, 1, 4, 1),
+            (2, 2, 11, 2),
+            (-2, -2, 12, 2),
+            (1, 1, 13, 2),
+            (-1, -1, 14, 2),
+        ):
+            send_z(src.at[z_at(own)], dst.at[slot], d, phase, group)
+
+    def reduce_relay(phase, src, dst, mid):
+        settle(recv_sem.at[phase, 3], dst, 1)
+        far = dst[8:9].astype(F32)
         for g, d in ((0, 4), (1, -4)):
             settle(recv_sem.at[phase, g], dst, 4)
             total = jnp.sum(dst[4 * g : 4 * g + 4].astype(F32), axis=0, keepdims=True)
-            mid[g : g + 1] = (total + src[pl.ds(z_at(d), 1)].astype(F32)).astype(BF16)
-            send_z(mid.at[g], dst.at[8 + g], d, phase, 2)
-
-    def wait_reduce_z(phase, src, dst):
-        settle(recv_sem.at[phase, 2], dst, 7)
-        return jnp.sum(dst[8:15].astype(F32), axis=0) + src[pl.ds(z, 1)].astype(F32)[0]
+            total = total + src[pl.ds(z_at(d), 1)].astype(F32)
+            total = total + jnp.where(side * d < 0, far, 0.0)
+            mid[g : g + 1] = total.astype(BF16)
+            send_z(mid.at[g], dst.at[9 + g], d, phase, 2)
+
+    def reduce_end(phase, src, dst):
+        settle(recv_sem.at[phase, 2], dst, 6)
+        return jnp.sum(dst[9:15].astype(F32), axis=0) + src[pl.ds(z, 1)].astype(F32)[0]
 
     def send_f(phase, src, dst):
         def step(i, c):
@@ -253,6 +292,22 @@
 
     def wait_f(phase, buf):
         settle(recv_sem.at[phase, 0], buf, NF - 1)
+
+    results = [
+        pltpu.make_async_copy(a, b, out_sem.at[i])
+        for i, (a, b) in enumerate(
+            (
+                (grad_fc_v, grad_fc_hbm),
+                (grad_gain_v, grad_gain_hbm),
+                (grad_gate_v, grad_gate_hbm),
+                (grad_up_v, grad_up_hbm),
+                (grad_down_v, grad_down_hbm),
+            )
+        )
+    ]
+
+    def leave(i):
+        results[i].start()
 
     mine_z = pl.ds(z, 1)
     mine_f = pl.ds(f, 1)
@@ -280,7 +335,7 @@
     r = iota((256, 1), 0)
     r = jnp.where(r < 128, r, r - 8)
     receiver = (r * 205) >> 11
-    goal = seat((receiver - z + NZ) % NZ) + r - receiver * PIECE
+    goal = seat((receiver - z + NZ) % NZ, side) + r - receiver * PIECE
     goal = jnp.where(receiver < NZ, goal, -1)
     spread = jnp.where(goal == iota((256, 3 * 128), 1), 1.0, 0.0).astype(BF16)
     tails = dot(line, spread)
@@ -289,19 +344,18 @@
         a_src[v, :, 256:384] = (base[:, 256:384] + tails[:, 128 * v : 128 * v + 128]).astype(BF16)
     a_buf[mine_z] = a_src[2:3]
 
-    pl.semaphore_wait(barrier, len(Z_PEERS) + NF - 1)
-    relay = gather_z(0, a_buf, a_src.at[0], a_src.at[1])
-
-    fc_w[...] = jnp.zeros_like(fc_w)
-    gate_w[...] = jnp.zeros_like(gate_w)
-    up_w[...] = jnp.zeros_like(up_w)
-    down_w[...] = jnp.zeros_like(down_w)
-    for load in loads[4:]:
-        load.wait()
-    fc_w[0:DB, 0:DB] = fc_v[...]
-    gate_w[0:DB, 0:FB] = gate_v[...]
-    up_w[0:DB, 0:FB] = up_v[...]
-    down_w[0:DB, 0:FB] = down_v[...]
+    def prepare():
+        fc_w[...] = jnp.zeros_like(fc_w)
+        gate_w[...] = jnp.zeros_like(gate_w)
+        up_w[...] = jnp.zeros_like(up_w)
+        down_w[...] = jnp.zeros_like(down_w)
+        for load in loads[4:]:
+            load.wait()
+        fc_w[0:DB, 0:DB] = fc_v[...]
+        gate_w[0:DB, 0:FB] = gate_v[...]
+        up_w[0:DB, 0:FB] = up_v[...]
+        down_w[0:DB, 0:FB] = down_v[...]
+
     gain = gain_v[...].reshape(1, DB)
     gain = jnp.concatenate([gain, jnp.ones((1, DP - DB), F32)], axis=1)
     packed_row = iota((16, 128), 0)
@@ -310,8 +364,11 @@
         gain[:, 0:128],
         jnp.where(packed_row < 8, gain[:, 128:256], gain[:, 256:384]),
     )
-    relay()
-    wait_gather_z(0, a_buf)
+    pl.semaphore_wait(barrier, len(Z_PEERS) + NF - 1)
+    gather_start(0, a_buf, a_src.at[0], a_src.at[1])
+    prepare()
+    gather_relay(0, a_buf)
+    gather_end(0, a_buf)
 
     slots = a_buf[...].reshape(NZ * CAP, DP)
     before = jnp.where(iota((256, 256), 1) // CAP < iota((256, 256), 0) // CAP, 1.0, 0.0).astype(BF16)
@@ -320,7 +377,7 @@
     place = (iota((256, ROWS), 0) % CAP).astype(F32)
     goes = iota((256, ROWS), 1).astype(F32) == start + place
     select = jnp.where((place < count) & goes, 1.0, 0.0).astype(BF16)
-    group = seat((z - lax.div(iota((256, 1), 0), CAP) + NZ) % NZ) % 128
+    group = seat((z - lax.div(iota((256, 1), 0), CAP) + NZ) % NZ, side) % 128
     lane = iota((256, 128), 1)
     meant = (lane >= group) & (lane < group + PIECE) | (lane < 64)
     tail = jnp.where(meant, slots[:, 256:384].astype(F32), 0.0).astype(BF16)
@@ -357,71 +414,106 @@
     sq_high, sq_low = split(squares)
     lane = iota((ROWS, FP), 1)
     gate_part = jnp.where(lane == META, sq_high, jnp.where(lane == META + 1, sq_low, gate_part))
-    d1_src[...] = jnp.concatenate(
-        [gate_part.reshape(NZ, 8, FP), up_part.reshape(NZ, 8, FP)], axis=1
-    ).astype(BF16)
-    reduce_z(3, d1_src, d1_dst, d1_mid)
-    both = wait_reduce_z(3, d1_src, d1_dst)
-    gate_sum, up_sum = both[0:8], both[8:16]
-    lane8 = iota((8, FP), 1)
-    square = jnp.sum(
-        jnp.where((lane8 == META) | (lane8 == META + 1), gate_sum, 0.0), axis=1, keepdims=True
-    )
+    d1a_src[...] = twin(gate_part[:, CUT:], up_part[:, CUT:]).astype(BF16)
+    reduce_start(3, d1a_src, d1a_dst)
+    d1b_src[...] = twin(gate_part[:, :CUT], up_part[:, :CUT]).astype(BF16)
+    reduce_start(4, d1b_src, d1b_dst)
+    reduce_relay(3, d1a_src, d1a_dst, d1a_mid)
+    reduce_relay(4, d1b_src, d1b_dst, d1b_mid)
+
+    both_a = reduce_end(3, d1a_src, d1a_dst)
+    lane_a = iota((8, FP - CUT), 1) + CUT
+    real = lane_a < FB
+    spare = (lane_a == META) | (lane_a == META + 1)
+    square = jnp.sum(jnp.where(spare, both_a[0:8], 0.0), axis=1, keepdims=True)
     inverse = lax.rsqrt(square / D + EPS)
-    real = lane8 < FB
-    gate_pre = jnp.where(real, gate_sum * inverse, 0.0)
-    up_pre = up_sum * inverse
-    sig = jax.nn.sigmoid(gate_pre)
-    act = gate_pre * sig * up_pre
-    d2_buf[mine_z] = fold(act).astype(BF16)
-    gather_z(4, d2_buf)()
-    wait_gather_z(4, d2_buf)
-
-    act_all = unfold(d2_buf[...].astype(F32)).astype(BF16)
-    down_part = dot(act_all, down_w[...], 1, 1) - target_part
+    gate_a = jnp.where(real, both_a[0:8] * inverse, 0.0)
+    up_a = both_a[8:16] * inverse
+    sig_a = jax.nn.sigmoid(gate_a)
+    d2a_buf[mine_z] = fold(gate_a * sig_a * up_a).astype(BF16)
+    gather_start(5, d2a_buf)
+
+    both_b = reduce_end(4, d1b_src, d1b_dst)
+    gate_b = both_b[0:8] * inverse
+    up_b = both_b[8:16] * inverse
+    sig_b = jax.nn.sigmoid(gate_b)
+    d2b_buf[mine_z] = fold(gate_b * sig_b * up_b).astype(BF16)
+    gather_start(6, d2b_buf)
+    gather_relay(5, d2a_buf)
+    gather_relay(6, d2b_buf)
+
+    gather_end(5, d2a_buf)
+    act_a = unfold(d2a_buf[...].astype(F32), FP - CUT).astype(BF16)
+    down_part = dot(act_a, down_w[:, CUT:], 1, 1) - target_part
+    gather_end(6, d2b_buf)
+    act_b = unfold(d2b_buf[...].astype(F32), CUT).astype(BF16)
+    down_part = down_part + dot(act_b, down_w[:, :CUT], 1, 1)
     pack_into(e1_src, (down_part[:, 0:128], down_part[:, 128:256], down_part[:, 256:384], none))
     e1_dst[mine_f] = e1_src[mine_f]
-    send_f(5, e1_src, e1_dst)
-    wait_f(5, e1_dst)
+    send_f(7, e1_src, e1_dst)
+    wait_f(7, e1_dst)
 
     loss_grad = (mixed + total_f(e1_dst)) * SCALE
     e2_buf[mine_f] = loss_grad.astype(BF16).reshape(1, 16, 128)
-    send_f(6, None, e2_buf)
-    wait_f(6, e2_buf)
+    send_f(8, None, e2_buf)
+    wait_f(8, e2_buf)
 
     loss_all = jnp.concatenate(unpack(e2_buf[...].astype(F32))[:3], axis=1).astype(BF16)
-    back_part = dot(loss_all, down_w[...])
-    f1_src[...] = fold(back_part).astype(BF16)
-    reduce_z(7, f1_src, f1_dst, f1_mid)
-    grad_down_ref[...] = dot(loss_all, act_all, 0, 0)[0:DB, 0:FB]
-    back_act = wait_reduce_z(7, f1_src, f1_dst)
-    back_act = unfold(back_act.reshape(1, 16, 512))
-    back_gate = back_act * up_pre * sig * (1.0 + gate_pre * (1.0 - sig))
-    back_up = back_act * gate_pre * sig
-    inner = inverse * inverse / D * jnp.sum(
-        jnp.where(real, back_gate * gate_pre + back_up * up_pre, 0.0), axis=1, keepdims=True
-    )
+    f1b_src[...] = fold(dot(loss_all, down_w[:, :CUT])).astype(BF16)
+    reduce_start(9, f1b_src, f1b_dst)
+    f1a_src[...] = fold(dot(loss_all, down_w[:, CUT:])).astype(BF16)
+    reduce_start(10, f1a_src, f1a_dst)
+    reduce_relay(9, f1b_src, f1b_dst, f1b_mid)
+    reduce_relay(10, f1a_src, f1a_dst, f1a_mid)
+
+    def back(back_act, gate_pre, up_pre, sig):
+        back_gate = back_act * up_pre * sig * (1.0 + gate_pre * (1.0 - sig))
+        back_up = back_act * gate_pre * sig
+        return back_gate, back_up, back_gate * gate_pre + back_up * up_pre
+
+    back_b = unfold(reduce_end(9, f1b_src, f1b_dst).reshape(1, 16, 256), CUT)
+    bg, bu, terms_b = back(back_b, gate_b, up_b, sig_b)
+    f2b_buf[mine_z] = twin(bg * inverse, bu * inverse).astype(BF16)
+    gather_start(11, f2b_buf)
+
+    back_a = unfold(reduce_end(10, f1a_src, f1a_dst).reshape(1, 16, 256), FP - CUT)
+    bg, bu, terms_a = back(back_a, gate_a, up_a, sig_a)
+    inner = jnp.sum(jnp.where(real, terms_a, 0.0), axis=1, keepdims=True)
+    inner = inverse * inverse / D * (inner + jnp.sum(terms_b, axis=1, keepdims=True))
     in_high, in_low = split(inner)
-    back_gate = jnp.where(real, back_gate * inverse, 0.0)
-    back_gate = jnp.where(lane8 == META, in_high, jnp.where(lane8 == META + 1, in_low, back_gate))
-    back_up = jnp.where(real, back_up * inverse, 0.0)
-    f2_buf[mine_z] = jnp.concatenate([back_gate, back_up], axis=0).astype(BF16).reshape(1, 16, FP)
-    gather_z(8, f2_buf)()
-    wait_gather_z(8, f2_buf)
-
-    back_both = f2_buf[...].astype(F32)
-    bg_all = back_both[:, 0:8].reshape(ROWS, FP)
-    bu_all = back_both[:, 8:16].reshape(ROWS, FP).astype(BF16)
+    bg = jnp.where(real, bg * inverse, 0.0)
+    bg = jnp.where(lane_a == META, in_high, jnp.where(lane_a == META + 1, in_low, bg))
+    bu = jnp.where(real, bu * inverse, 0.0)
+    f2a_buf[mine_z] = twin(bg, bu).astype(BF16)
+    gather_start(12, f2a_buf)
+    gather_relay(11, f2b_buf)
+    gather_relay(12, f2a_buf)
+    grad_down_v[:, 0:CUT] = dot(loss_all, act_b, 0, 0)[0:DB]
+    grad_down_v[:, CUT:FB] = dot(loss_all, act_a, 0, 0)[0:DB, 0 : FB - CUT]
+    leave(4)
+
+    gather_end(11, f2b_buf)
+    back_both = f2b_buf[...].astype(F32)
+    bg_b = back_both[:, 0:8].reshape(ROWS, CUT).astype(BF16)
+    bu_b = back_both[:, 8:16].reshape(ROWS, CUT).astype(BF16)
+    norm_part = dot(bg_b, gate_w[:, :CUT], 1, 1) + dot(bu_b, up_w[:, :CUT], 1, 1)
+    gather_end(12, f2a_buf)
+    back_both = f2a_buf[...].astype(F32)
+    bg_a = back_both[:, 0:8].reshape(ROWS, FP - CUT)
+    bu_a = back_both[:, 8:16].reshape(ROWS, FP - CUT).astype(BF16)
     lane = iota((ROWS, 128), 1) + 768
-    inner_tile = jnp.where((lane == META) | (lane == META + 1), bg_all[:, 768:896], 0.0)
-    bg_all = bg_all.astype(BF16)
-    norm_part = dot(bg_all, gate_w[...], 1, 1) + dot(bu_all, up_w[...], 1, 1)
+    inner_tile = jnp.where((lane == META) | (lane == META + 1), bg_a[:, 768 - CUT :], 0.0)
+    bg_a = bg_a.astype(BF16)
+    norm_part = norm_part + dot(bg_a, gate_w[:, CUT:], 1, 1) + dot(bu_a, up_w[:, CUT:], 1, 1)
     pack_into(g1_src, (norm_part[:, 0:128], norm_part[:, 128:256], norm_part[:, 256:384], inner_tile))
     g1_dst[mine_f] = g1_src[mine_f]
-    send_f(9, g1_src, g1_dst)
-    grad_gate_ref[...] = dot(h, bg_all, 0, 0)[0:DB, 0:FB].astype(BF16)
-    grad_up_ref[...] = dot(h, bu_all, 0, 0)[0:DB, 0:FB].astype(BF16)
-    wait_f(9, g1_dst)
+    send_f(13, g1_src, g1_dst)
+    for grad, back_a, back_b in ((grad_gate_v, bg_a, bg_b), (grad_up_v, bu_a, bu_b)):
+        grad[:, 0:CUT] = dot(h, back_b, 0, 0)[0:DB].astype(BF16)
+        grad[:, CUT:FB] = dot(h, back_a, 0, 0)[0:DB, 0 : FB - CUT].astype(BF16)
+    leave(2)
+    leave(3)
+    wait_f(13, g1_dst)
 
     back_norm = total_f(g1_dst)
     inner_col = jnp.sum(jnp.where(packed_row >= 12, back_norm, 0.0), axis=1, keepdims=True)
@@ -435,29 +527,49 @@
     for k in range(3):
         back_mix = jnp.where(packed_row == 12 + k, gain_sums[k], back_mix)
     g2_buf[mine_f] = back_mix.astype(BF16).reshape(1, 16, 128)
-    send_f(10, None, g2_buf)
-    wait_f(10, g2_buf)
+    send_f(14, None, g2_buf)
+    wait_f(14, g2_buf)
 
     mix_packed = g2_buf[...].astype(F32)
     mix_all = jnp.concatenate(unpack(mix_packed)[:3], axis=1).astype(BF16)
-    grad_fc_ref[...] = dot(live, mix_all, 0, 0)[0:DB, 0:DB]
+    grad_fc_v[...] = dot(live, mix_all, 0, 0)[0:DB, 0:DB]
+    leave(0)
     gain_total = jnp.sum(mix_packed, axis=0)
-    for k in range(3):
-        grad_gain_ref[:, 128 * k : 128 * k + 128] = gain_total[12 + k : 13 + k]
-
-    for phase, buf in ((0, a_buf), (3, d1_dst), (4, d2_buf), (7, f1_dst), (8, f2_buf)):
+    gain_line = jnp.concatenate([gain_total[12 + k : 13 + k] for k in range(3)], axis=1)
+    grad_gain_v[...] = gain_line[:, 0:DB].reshape(DB)
+    leave(1)
+
+    for phase, buf in (
+        (0, a_buf),
+        (3, d1a_dst),
+        (4, d1b_dst),
+        (5, d2a_buf),
+        (6, d2b_buf),
+        (9, f1b_dst),
+        (10, f1a_dst),
+        (11, f2b_buf),
+        (12, f2a_buf),
+    ):
         settle(send_sem.at[phase], buf, NZ - 1)
-    for phase, buf in ((1, b1_dst), (2, b2_buf), (5, e1_dst), (6, e2_buf), (9, g1_dst), (10, g2_buf)):
+    for phase, buf in ((1, b1_dst), (2, b2_buf), (7, e1_dst), (8, e2_buf), (13, g1_dst), (14, g2_buf)):
         settle(send_sem.at[phase], buf, NF - 1)
+    for result in results:
+        result.wait()
 
 
 def store_kernel(*refs):
-    sems = refs[10]
-    copies = [pltpu.make_async_copy(refs[i], refs[5 + i], sems.at[i]) for i in range(5)]
-    for copy in copies:
-        copy.start()
-    for copy in copies:
-        copy.wait()
+    sources, targets, held = refs[0:5], refs[5:10], refs[10:15]
+    in_sem, out_sem = refs[15:17]
+    order = (4, 2, 3, 0, 1)
+    loads = {i: pltpu.make_async_copy(sources[i], held[i], in_sem.at[i]) for i in order}
+    stores = {i: pltpu.make_async_copy(held[i], targets[i], out_sem.at[i]) for i in order}
+    for i in order:
+        loads[i].start()
+    for i in order:
+        loads[i].wait()
+        stores[i].start()
+    for i in order:
+        stores[i].wait()
 
 
 def shards(
@@ -476,7 +588,7 @@
     xy = pltpu.VMEM((NF, 16, 128), BF16)
     shapes = (
         jax.ShapeDtypeStruct((DB, DB), F32),
-        jax.ShapeDtypeStruct((1, DP), F32),
+        jax.ShapeDtypeStruct((DB,), F32),
         jax.ShapeDtypeStruct((DB, FB), BF16),
         jax.ShapeDtypeStruct((DB, FB), BF16),
         jax.ShapeDtypeStruct((DB, FB), F32),
@@ -485,7 +597,7 @@
         kernel,
         out_shape=shapes,
         in_specs=[pl.BlockSpec(memory_space=pltpu.SMEM)] + [hbm] * 8,
-        out_specs=[vmem] * 5,
+        out_specs=[hbm] * 5,
         scratch_shapes=[
             pltpu.VMEM((CAP, 160), BF16),
             pltpu.VMEM((CAP, 160), BF16),
@@ -504,23 +616,37 @@
             xy,
             xy,
             xy,
-            pltpu.VMEM((NZ, 16, FP), BF16),
-            pltpu.VMEM((NZ - 1, 16, FP), BF16),
-            pltpu.VMEM((2, 16, FP), BF16),
-            pltpu.VMEM((NZ, 16, 512), BF16),
-            xy,
-            xy,
-            xy,
-            pltpu.VMEM((NZ, 16, 512), BF16),
-            pltpu.VMEM((NZ - 1, 16, 512), BF16),
-            pltpu.VMEM((2, 16, 512), BF16),
-            pltpu.VMEM((NZ, 16, FP), BF16),
-            xy,
-            xy,
-            xy,
+            pltpu.VMEM((NZ, 16, FP - CUT), BF16),
+            pltpu.VMEM((NZ - 1, 16, FP - CUT), BF16),
+            pltpu.VMEM((2, 16, FP - CUT), BF16),
+            pltpu.VMEM((NZ, 16, CUT), BF16),
+            pltpu.VMEM((NZ - 1, 16, CUT), BF16),
+            pltpu.VMEM((2, 16, CUT), BF16),
+            pltpu.VMEM((NZ, 16, 256), BF16),
+            pltpu.VMEM((NZ, 16, 256), BF16),
+            xy,
+            xy,
+            xy,
+            pltpu.VMEM((NZ, 16, 256), BF16),
+            pltpu.VMEM((NZ - 1, 16, 256), BF16),
+            pltpu.VMEM((2, 16, 256), BF16),
+            pltpu.VMEM((NZ, 16, 256), BF16),
+            pltpu.VMEM((NZ - 1, 16, 256), BF16),
+            pltpu.VMEM((2, 16, 256), BF16),
+            pltpu.VMEM((NZ, 16, FP - CUT), BF16),
+            pltpu.VMEM((NZ, 16, CUT), BF16),
+            xy,
+            xy,
+            xy,
+            pltpu.VMEM((DB, DB), F32),
+            pltpu.VMEM((DB,), F32),
+            pltpu.VMEM((DB, FB), BF16),
+            pltpu.VMEM((DB, FB), BF16),
+            pltpu.VMEM((DB, FB), F32),
             pltpu.SemaphoreType.DMA((8,)),
-            pltpu.SemaphoreType.DMA((11,)),
-            pltpu.SemaphoreType.DMA((11, 3)),
+            pltpu.SemaphoreType.DMA((5,)),
+            pltpu.SemaphoreType.DMA((15,)),
+            pltpu.SemaphoreType.DMA((15, 4)),
         ],
         compiler_params=pltpu.CompilerParams(
             collective_id=0, has_side_effects=True, vmem_limit_bytes=56 << 20
@@ -540,14 +666,15 @@
     grad_fc, grad_gain, grad_gate, grad_up, grad_down = pl.pallas_call(
         store_kernel,
         out_shape=shapes,
-        in_specs=[vmem] * 5,
+        in_specs=[hbm] * 5,
         out_specs=[hbm] * 5,
-        scratch_shapes=[pltpu.SemaphoreType.DMA((5,))],
+        scratch_shapes=[pltpu.VMEM(shape.shape, shape.dtype) for shape in shapes]
+        + [pltpu.SemaphoreType.DMA((5,)), pltpu.SemaphoreType.DMA((5,))],
         name="store_results",
     )(*found)
     return (
         grad_fc.reshape(2, DB // 2, DB),
-        grad_gain[0, :DB],
+        grad_gain,
         grad_gate,
         grad_up,
         grad_down.T,

time: 116 us -> 110 us (0.948)
  Pallas kernels: 113 us -> 108 us
  local copies, waits for them, and re-layouts: 1.27 us -> 0 us
    pallas_call x1, Pallas kernels: 110 us -> 105 us  [shards(): pl.pallas_call(kernel, out_shape=shapes, in_specs=[pl.BlockSpec(memory_sp...]
    slice x1 -> x0, local copies, waits for them, and re-layouts: 1.27 us -> none  [shards(): grad_gain[0, :DB]]
where the time goes in v3:
time: 110 us
  Pallas kernels  108 us (98%)
  between operations  1.29 us (1%)
    pallas_call x1, Pallas kernels, shards(): pl.pallas_call(kernel, out_shape=shapes, in_specs=[pl.BlockSpec(memory_sp...  105 us
    pallas_call x1, Pallas kernels, shards(): pl.pallas_call(store_kernel, out_shape=shapes, in_specs=[hbm] * 5, out_sp...  2.88 us

profile of v3, /device:TPU:1, one launch (start us, length us, event | category | flops | bytes accessed | tf_op | source)
XLA Modules:
  0.0 109.6 jit_solution(16167724998790291251)
XLA Ops:
  1.3 105.4 %draft_layer.1 = (f32[320,320]{1,0:T(8,128)}, f32[320]{0:T(512)}, bf16[320,800]{1,0:T(8,128)(2,1)}, bf16[320,800]{1,0:T(8,128)(2,1)}, f32[320,800]{1,0:T(8,128)}) custom-call(s32[1]{0:T(128)S(6)} %copy.14.counts_ref, bf16[16,160]{1,0:T(8,128)(2,1)} %hidden_hbm.1, bf16[16,160]{1,0:T(8,128)(2,1)} %embed_hbm.1, bf16[16,5120]{1,0:T(8,128)(2,1)} %target_hbm.1, ...), custom_call_target="tpu_custom_call" | custom-call | tf_op jit(solution)/shard_map/draft_layer/pallas_call | solution.py:596
  106.7 2.9 %store_results.1 = (f32[320,320]{1,0:T(8,128)}, f32[320]{0:T(512)}, bf16[320,800]{1,0:T(8,128)(2,1)}, bf16[320,800]{1,0:T(8,128)(2,1)}, f32[320,800]{1,0:T(8,128)}) custom-call(f32[320,320]{1,0:T(8,128)} %get-tuple-element.15.refs_0_, f32[320]{0:T(512)} %get-tuple-element.16.refs_1_, bf16[320,800]{1,0:T(8,128)(2,1)} %get-tuple-element.17.refs_2_, ...), custom_call_target="tpu_custom_call" | custom-call | tf_op jit(solution)/shard_map/store_results/pallas_call | solution.py:666

commit v4 on v3

--- a/solution.py
+++ b/solution.py
@@ -20,6 +20,10 @@
 CUT = 384
 META = 832
 EPS = 1e-06
+F_ORDER = sorted(
+    ((x, y, c) for x in range(4) for y in range(4) for c in range(2) if x + y + c),
+    key=lambda at: -min(at[0], 4 - at[0]) - min(at[1], 4 - at[1]),
+)
 SCALE = 1.0 / math.sqrt(ROWS)
 F32 = jnp.float32
 BF16 = jnp.bfloat16
@@ -170,14 +174,11 @@
     def z_at(offset):
         return lax.rem(z + (offset + NZ), NZ)
 
-    def far_first(k):
-        return lax.rem(10 - lax.div(k * (k + 1), 2), 4)
-
     def f_peer(i):
-        j = lax.div(i, 2)
-        x = lax.rem(f_x + far_first(lax.div(j, 4)), 4)
-        y = lax.rem(f_y + far_first(lax.rem(j, 4)), 4)
-        c = lax.rem(f_c + 1 + i, 2)
+        dx, dy, dc = F_ORDER[i]
+        x = lax.rem(f_x + dx, 4)
+        y = lax.rem(f_y + dy, 4)
+        c = f_c if dc == 0 else 1 - f_c
         return x * 8 + y * 2 + c
 
     loads = [
@@ -206,7 +207,8 @@
 
     for d in Z_PEERS:
         pl.semaphore_signal(barrier, inc=1, device_id=(z_at(d), f), device_id_type=MESH)
-    lax.fori_loop(0, NF - 1, greet_f, 0)
+    for i in range(NF - 1):
+        greet_f(i, 0)
 
     def send_z(src, dst, d, phase, group):
         pltpu.make_async_remote_copy(
@@ -253,12 +255,12 @@
             (-5, -1, 5, 1),
             (3, -1, 0, 0),
             (-3, 1, 4, 1),
-            (2, 2, 11, 2),
-            (-2, -2, 12, 2),
-            (1, 1, 13, 2),
-            (-1, -1, 14, 2),
         ):
             send_z(src.at[z_at(own)], dst.at[slot], d, phase, group)
+
+    def reduce_near(phase, src, dst):
+        for d, slot in ((2, 11), (-2, 12), (1, 13), (-1, 14)):
+            send_z(src.at[z_at(d)], dst.at[slot], d, phase, 2)
 
     def reduce_relay(phase, src, dst, mid):
         settle(recv_sem.at[phase, 3], dst, 1)
@@ -288,7 +290,8 @@
             ).start()
             return c
 
-        lax.fori_loop(0, NF - 1, step, 0)
+        for i in range(NF - 1):
+            step(i, 0)
 
     def wait_f(phase, buf):
         settle(recv_sem.at[phase, 0], buf, NF - 1)
@@ -418,6 +421,8 @@
     reduce_start(3, d1a_src, d1a_dst)
     d1b_src[...] = twin(gate_part[:, :CUT], up_part[:, :CUT]).astype(BF16)
     reduce_start(4, d1b_src, d1b_dst)
+    reduce_near(3, d1a_src, d1a_dst)
+    reduce_near(4, d1b_src, d1b_dst)
     reduce_relay(3, d1a_src, d1a_dst, d1a_mid)
     reduce_relay(4, d1b_src, d1b_dst, d1b_mid)
 
@@ -463,6 +468,8 @@
     reduce_start(9, f1b_src, f1b_dst)
     f1a_src[...] = fold(dot(loss_all, down_w[:, CUT:])).astype(BF16)
     reduce_start(10, f1a_src, f1a_dst)
+    reduce_near(9, f1b_src, f1b_dst)
+    reduce_near(10, f1a_src, f1a_dst)
     reduce_relay(9, f1b_src, f1b_dst, f1b_mid)
     reduce_relay(10, f1a_src, f1a_dst, f1a_mid)
 

time: 110 us -> 107 us (0.973)
  Pallas kernels: 108 us -> 106 us
    pallas_call x1, Pallas kernels: 105 us -> 103 us  [shards(): pl.pallas_call(kernel, out_shape=shapes, in_specs=[pl.BlockSpec(memory_sp...]
where the time goes in v4:
time: 107 us
  Pallas kernels  106 us (99%)
  between operations  1.29 us (1%)
    pallas_call x1, Pallas kernels, shards(): pl.pallas_call(kernel, out_shape=shapes, in_specs=[pl.BlockSpec(memory_sp...  103 us
    pallas_call x1, Pallas kernels, shards(): pl.pallas_call(store_kernel, out_shape=shapes, in_specs=[hbm] * 5, out_sp...  2.88 us

profile of v4, /device:TPU:1, one launch (start us, length us, event | category | flops | bytes accessed | tf_op | source)
XLA Modules:
  0.0 107.2 jit_solution(18303229276982267187)
XLA Ops:
  1.3 103.0 %draft_layer.1 = (f32[320,320]{1,0:T(8,128)}, f32[320]{0:T(512)}, bf16[320,800]{1,0:T(8,128)(2,1)}, bf16[320,800]{1,0:T(8,128)(2,1)}, f32[320,800]{1,0:T(8,128)}) custom-call(s32[1]{0:T(128)S(6)} %copy.14.counts_ref, bf16[16,160]{1,0:T(8,128)(2,1)} %hidden_hbm.1, bf16[16,160]{1,0:T(8,128)(2,1)} %embed_hbm.1, bf16[16,5120]{1,0:T(8,128)(2,1)} %target_hbm.1, ...), custom_call_target="tpu_custom_call" | custom-call | tf_op jit(solution)/shard_map/draft_layer/pallas_call | solution.py:603
  104.3 2.9 %store_results.1 = (f32[320,320]{1,0:T(8,128)}, f32[320]{0:T(512)}, bf16[320,800]{1,0:T(8,128)(2,1)}, bf16[320,800]{1,0:T(8,128)(2,1)}, f32[320,800]{1,0:T(8,128)}) custom-call(f32[320,320]{1,0:T(8,128)} %get-tuple-element.15.refs_0_, f32[320]{0:T(512)} %get-tuple-element.16.refs_1_, bf16[320,800]{1,0:T(8,128)(2,1)} %get-tuple-element.17.refs_2_, ...), custom_call_target="tpu_custom_call" | custom-call | tf_op jit(solution)/shard_map/store_results/pallas_call | solution.py:673

commit v5 on v4

--- a/solution.py
+++ b/solution.py
@@ -17,7 +17,7 @@
 FB = 800
 FP = 896
 PIECE = DB // NF
-CUT = 384
+CUT = 512
 META = 832
 EPS = 1e-06
 F_ORDER = sorted(
@@ -389,8 +389,8 @@
     fc_part = dot(live, fc_w[...])
     none = jnp.zeros((ROWS, 128), F32)
     pack_into(b1_src, (fc_part[:, 0:128], fc_part[:, 128:256], fc_part[:, 256:384], none))
+    send_f(1, b1_src, b1_dst)
     b1_dst[mine_f] = b1_src[mine_f]
-    send_f(1, b1_src, b1_dst)
     col = iota((128, DP), 1)
     row = iota((128, DP), 0) - 64
     inside = (row >= 0) & (row < 6 * PIECE)
@@ -412,14 +412,13 @@
     plain = h / gain
     squares = jnp.sum(plain * plain, axis=1, keepdims=True)
     h = h.astype(BF16)
-    gate_part = dot(h, gate_w[...])
-    up_part = dot(h, up_w[...])
     sq_high, sq_low = split(squares)
-    lane = iota((ROWS, FP), 1)
+    lane = iota((ROWS, FP - CUT), 1) + CUT
+    gate_part = dot(h, gate_w[:, CUT:])
     gate_part = jnp.where(lane == META, sq_high, jnp.where(lane == META + 1, sq_low, gate_part))
-    d1a_src[...] = twin(gate_part[:, CUT:], up_part[:, CUT:]).astype(BF16)
+    d1a_src[...] = twin(gate_part, dot(h, up_w[:, CUT:])).astype(BF16)
     reduce_start(3, d1a_src, d1a_dst)
-    d1b_src[...] = twin(gate_part[:, :CUT], up_part[:, :CUT]).astype(BF16)
+    d1b_src[...] = twin(dot(h, gate_w[:, :CUT]), dot(h, up_w[:, :CUT])).astype(BF16)
     reduce_start(4, d1b_src, d1b_dst)
     reduce_near(3, d1a_src, d1a_dst)
     reduce_near(4, d1b_src, d1b_dst)
@@ -454,8 +453,8 @@
     act_b = unfold(d2b_buf[...].astype(F32), CUT).astype(BF16)
     down_part = down_part + dot(act_b, down_w[:, :CUT], 1, 1)
     pack_into(e1_src, (down_part[:, 0:128], down_part[:, 128:256], down_part[:, 256:384], none))
+    send_f(7, e1_src, e1_dst)
     e1_dst[mine_f] = e1_src[mine_f]
-    send_f(7, e1_src, e1_dst)
     wait_f(7, e1_dst)
 
     loss_grad = (mixed + total_f(e1_dst)) * SCALE
@@ -513,8 +512,8 @@
     bg_a = bg_a.astype(BF16)
     norm_part = norm_part + dot(bg_a, gate_w[:, CUT:], 1, 1) + dot(bu_a, up_w[:, CUT:], 1, 1)
     pack_into(g1_src, (norm_part[:, 0:128], norm_part[:, 128:256], norm_part[:, 256:384], inner_tile))
+    send_f(13, g1_src, g1_dst)
     g1_dst[mine_f] = g1_src[mine_f]
-    send_f(13, g1_src, g1_dst)
     for grad, back_a, back_b in ((grad_gate_v, bg_a, bg_b), (grad_up_v, bu_a, bu_b)):
         grad[:, 0:CUT] = dot(h, back_b, 0, 0)[0:DB].astype(BF16)
         grad[:, CUT:FB] = dot(h, back_a, 0, 0)[0:DB, 0 : FB - CUT].astype(BF16)

time: 107 us -> 107 us (level)
  no operation moved by 1% of the time
where the time goes in v5:
time: 107 us
  Pallas kernels  106 us (99%)
  between operations  1.29 us (1%)
    pallas_call x1, Pallas kernels, shards(): pl.pallas_call(kernel, out_shape=shapes, in_specs=[pl.BlockSpec(memory_sp...  103 us
    pallas_call x1, Pallas kernels, shards(): pl.pallas_call(store_kernel, out_shape=shapes, in_specs=[hbm] * 5, out_sp...  2.88 us

profile of v5, /device:TPU:1, one launch (start us, length us, event | category | flops | bytes accessed | tf_op | source)
XLA Modules:
  0.0 107.0 jit_solution(16926608085511235719)
XLA Ops:
  1.3 102.8 %draft_layer.1 = (f32[320,320]{1,0:T(8,128)}, f32[320]{0:T(512)}, bf16[320,800]{1,0:T(8,128)(2,1)}, bf16[320,800]{1,0:T(8,128)(2,1)}, f32[320,800]{1,0:T(8,128)}) custom-call(s32[1]{0:T(128)S(6)} %copy.14.counts_ref, bf16[16,160]{1,0:T(8,128)(2,1)} %hidden_hbm.1, bf16[16,160]{1,0:T(8,128)(2,1)} %embed_hbm.1, bf16[16,5120]{1,0:T(8,128)(2,1)} %target_hbm.1, ...), custom_call_target="tpu_custom_call" | custom-call | tf_op jit(solution)/shard_map/draft_layer/pallas_call | solution.py:602
  104.1 2.9 %store_results.1 = (f32[320,320]{1,0:T(8,128)}, f32[320]{0:T(512)}, bf16[320,800]{1,0:T(8,128)(2,1)}, bf16[320,800]{1,0:T(8,128)(2,1)}, f32[320,800]{1,0:T(8,128)}) custom-call(f32[320,320]{1,0:T(8,128)} %get-tuple-element.15.refs_0_, f32[320]{0:T(512)} %get-tuple-element.16.refs_1_, bf16[320,800]{1,0:T(8,128)(2,1)} %get-tuple-element.17.refs_2_, ...), custom_call_target="tpu_custom_call" | custom-call | tf_op jit(solution)/shard_map/store_results/pallas_call | solution.py:672
